TPU v7x, 32 devices: a whole 2x2x4 slice. The times are simulated.
32 devices in a mesh: blk: 4 (over y, x), batch: 8 (over z, core).
Axes of the slice: x: 2, y: 2, z: 4, core: 2. Of those that a mesh axis runs over, the one named last changes fastest.
Arguments:
- inputs: bfloat16 [32, 512, 768], P('batch', 'blk'), may hold values from -6 to 6
- lengths: int32 [32], P('batch'), may hold values from 64 to 512, as said below
- positions: int32 [32, 80], P('batch'), may hold values from 0 to 511, as said below
- counts: int32 [32], P('batch'), may hold values from 40 to 80, as said below
- token_ids: int32 [32, 80], P('batch'), may hold values from 0 to 15359
- table: bfloat16 [15360, 768], replicated, may hold values from -6 to 6
- w_query: bfloat16 [768, 768], replicated, may hold values from -0.3125 to 0.3125
- b_query: bfloat16 [768], replicated, may hold values from -1.75 to 1.75
- w_key: bfloat16 [768, 768], replicated, may hold values from -0.21875 to 0.21875
- w_value: bfloat16 [768, 768], replicated, may hold values from -0.21875 to 0.21875
- b_value: bfloat16 [768], replicated, may hold values from -0.625 to 0.625
- w_out: bfloat16 [768, 768], replicated, may hold values from -1.75 to 1.75
- b_out: bfloat16 [768], replicated, may hold values from -3 to 3
- gain_one: bfloat16 [768], replicated, may hold values from 0.5 to 1.5
- shift_one: bfloat16 [768], replicated, may hold values from -1.75 to 1.75
- w_up: bfloat16 [768, 3072], replicated, may hold values from -0.21875 to 0.21875
- b_up: bfloat16 [3072], replicated, may hold values from -3 to 3
- w_down: bfloat16 [3072, 768], replicated, may hold values from -0.109375 to 0.109375
- b_down: bfloat16 [768], replicated, may hold values from -3 to 3
- gain_two: bfloat16 [768], replicated, may hold values from 0.5 to 1.5
- shift_two: bfloat16 [768], replicated, may hold values from -1.75 to 1.75
- cotangent: bfloat16 [32, 512, 768], P('batch', 'blk'), may hold values from -8 to 8
Outputs:
- outputs: bfloat16 [32, 512, 768], P('batch', 'blk')
- d_inputs: bfloat16 [32, 512, 768], P('batch', 'blk')
- grad_query: float32 [768, 768], P('batch')
- grad_query_bias: float32 [768], P('batch')
- grad_key: float32 [768, 768], P('batch')
- grad_value: float32 [768, 768], P('batch')
- grad_value_bias: float32 [768], P('batch')
- grad_out: float32 [768, 768], P('batch')
- grad_out_bias: float32 [768], P('batch')
- grad_gain_one: float32 [768], P('batch')
- grad_shift_one: float32 [768], P('batch')
- grad_up: float32 [768, 3072], P('batch')
- grad_up_bias: float32 [3072], P('batch')
- grad_down: float32 [3072, 768], P('batch')
- grad_down_bias: float32 [768], P('batch')
- grad_gain_two: float32 [768], P('batch')
- grad_shift_two: float32 [768], P('batch')
Inputs may be any that keep to these rules, and one draw needn't show every extreme that they name: `lengths`: in each group of 4 pages that one index of batch holds, at least one page has length 512. The 80 positions listed for a page are distinct; entries at or past the page's count are present but unused. `counts`: some page has exactly 80 masked positions.
All inputs are finite; a program needn't handle non-finite values.
Results may differ from a plain program's by a relative error of at most 0.02.
Values may be sent and summed in bfloat16 or wider, within the bound.
No kernel may reach another device: no remote copies, remote signals or barrier semaphores. Data moves between devices by JAX's collectives and lax.ppermute only.
A program may use at most 192 MiB of HBM per device.

v0:
```python
import functools

import jax
import jax.numpy as jnp
from jax import lax
from jax.experimental import pallas as pl
from jax.experimental.pallas import tpu as pltpu
from jax.sharding import PartitionSpec as P

HEADS = 12
HD = 64
SCALE = 0.125
NEGATIVE = -1e30
EPSILON = 1e-12
BF = jnp.bfloat16
F32 = jnp.float32
MIB = 1024 * 1024
GROUP = 16
PARTS = 8
DOWN_Z = 80
B_QUERY, B_VALUE, B_OUT, B_DOWN, GAIN_ONE, SHIFT_ONE, GAIN_TWO, SHIFT_TWO, B_UP = range(9)


def nn(a, b):
    return lax.dot_general(a, b, (((1,), (0,)), ((), ())), preferred_element_type=F32)


def nt(a, b):
    return lax.dot_general(a, b, (((1,), (1,)), ((), ())), preferred_element_type=F32)


def tn(a, b):
    return lax.dot_general(a, b, (((0,), (0,)), ((), ())), preferred_element_type=F32)


def head_lanes(shape, which):
    lane = lax.broadcasted_iota(jnp.int32, shape, 1)
    return (lane >= HD) if which else (lane < HD)


def norm_parts(v):
    width = v.shape[-1]
    centre = jnp.sum(v, axis=-1, keepdims=True) * (1.0 / width)
    centred = v - centre
    spread = jnp.sum(centred * centred, axis=-1, keepdims=True) * (1.0 / width)
    rstd = lax.rsqrt(spread + EPSILON)
    return centred * rstd, rstd


def norm_back(c2, n, rstd):
    width = c2.shape[-1]
    a = jnp.sum(c2, axis=-1, keepdims=True) * (1.0 / width)
    b = jnp.sum(c2 * n, axis=-1, keepdims=True) * (1.0 / width)
    return (c2 - a - n * b) * rstd


def colsum(v):
    return jnp.sum(v, axis=0, keepdims=True)


def wide_row(ref):
    return ref[...].astype(F32).reshape(1, ref.shape[0])


def block(i, size):
    return pl.ds(pl.multiple_of(i * size, size), size)


def own_blk():
    return lax.axis_index("blk")


def own_core():
    return lax.rem(lax.axis_index("batch"), 2)


def first_bit():
    return jnp.where(own_core() == 0, lax.rem(own_blk(), 2), lax.div(own_blk(), 2))


def second_bit():
    return jnp.where(own_core() == 0, lax.div(own_blk(), 2), lax.rem(own_blk(), 2))


def z_bits():
    z = lax.div(lax.axis_index("batch"), 2)
    return lax.rem(z, 2), lax.div(z, 2)


def fetch_kernel(ids_ref, counts_ref, spots_ref, table_ref, placed_ref, hit_ref, rows_ref, wide_ref, sel_ref, sem):
    slots = ids_ref.shape[1]
    me = own_blk()

    def start(j, carry):
        group = pl.multiple_of((ids_ref[me, j] // GROUP) * GROUP, GROUP)
        pltpu.make_async_copy(table_ref.at[pl.ds(group, GROUP), :], rows_ref.at[block(j, GROUP), :], sem).start()
        return carry

    lax.fori_loop(0, slots, start, 0, unroll=8)
    total = placed_ref.shape[0]
    spot = lax.broadcasted_iota(jnp.int32, (total, slots), 0)
    slot = lax.broadcasted_iota(jnp.int32, (total, slots), 1)
    hits = ((spots_ref[pl.ds(me, 1), :] == spot) & (slot < counts_ref[me])).astype(F32)
    hit_ref[...] = jnp.broadcast_to(jnp.sum(hits, axis=1, keepdims=True), hit_ref.shape)
    pltpu.make_async_copy(table_ref.at[pl.ds(0, slots * GROUP), :], rows_ref, sem).wait()
    wide_ref[...] = rows_ref[...].astype(F32)

    def select(j, carry):
        at = j * GROUP + lax.rem(ids_ref[me, j], GROUP)
        sel_ref[pl.ds(j, 1), :] = wide_ref[pl.ds(at, 1), :]
        return carry

    lax.fori_loop(0, slots, select, 0, unroll=8)
    placed_ref[...] = nn(hits.astype(BF), sel_ref[...].astype(BF)).astype(BF)


def attend_kernel(
    lengths_ref, inputs_ref, p1_ref, p2_ref, p3_ref, placed_ref, hit_ref, bq_ref, bv_ref, bo_ref,
    wq_ref, wk_ref, wv_ref, wo_ref,
    x_t_ref, q_ref, k_ref, v_ref, att_ref, max_ref, sum_ref, n_ref, rstd_ref,
    x_ref, att_rows,
):
    me = own_blk()
    length = lengths_ref[me]
    rows, width = x_ref.shape
    span = p1_ref.shape[0]
    for step, piece in enumerate((inputs_ref[me], p1_ref[...], p2_ref[...], p3_ref[...])):
        at = block(me ^ step, span)
        x_ref[at, :] = jnp.where(hit_ref[at, 0:1] > 0.5, placed_ref[at, :], piece)
    x_t_ref[...] = x_ref[...].T
    q = (nn(x_ref[...], wq_ref[...]) + wide_row(bq_ref)).astype(BF)
    q_ref[...] = (q.astype(F32) * SCALE).astype(BF)
    k_ref[...] = nn(x_ref[...], wk_ref[...]).astype(BF)
    v_ref[...] = (nn(x_ref[...], wv_ref[...]) + wide_row(bv_ref)).astype(BF)
    dead = jnp.where(lax.broadcasted_iota(jnp.int32, (rows, 1), 0) < length, 0.0, NEGATIVE)

    def pair(i, carry):
        lanes = block(i, 2 * HD)
        q2, k2 = q_ref[:, lanes], k_ref[:, lanes]
        v2t = v_ref[:, lanes].T
        for h in range(2):
            qm = jnp.where(head_lanes(q2.shape, h), q2, jnp.zeros_like(q2))
            s = nt(k2, qm) + dead
            top = jnp.max(s, axis=0, keepdims=True)
            p = jnp.exp(s - top)
            total = jnp.sum(p, axis=0, keepdims=True)
            o = nn(v2t[h * HD:(h + 1) * HD], p.astype(BF)) / total
            max_ref[2 * i + h] = top
            sum_ref[2 * i + h] = total
            att_ref[block(2 * i + h, HD), :] = o.astype(BF)
        att_rows[:, lanes] = att_ref[lanes, :].T
        return carry

    lax.fori_loop(0, HEADS // 2, pair, 0, unroll=True)
    branch = nn(att_rows[...], wo_ref[...]) + wide_row(bo_ref)
    n, rstd = norm_parts(x_ref[...].astype(F32) + branch)
    n_ref[...] = n
    rstd_ref[...] = jnp.broadcast_to(rstd, rstd_ref.shape)


def gelu_both(v):
    e = jnp.exp(v * v * -0.5)
    t = 1.0 / (1.0 + (0.3275911 * 0.7071067811865476) * jnp.abs(v))
    poly = t * (0.5 * 0.254829592 + t * (0.5 * -0.284496736 + t * (0.5 * 1.421413741 + t * (0.5 * -1.453152027 + t * (0.5 * 1.061405429)))))
    tail = poly * e
    phi = jnp.where(v >= 0, 1.0 - tail, tail)
    return v * phi, phi + v * (e * 0.3989422804014327)


def by_core(core, deal, keep, send):
    for c in range(2):

        @pl.when(core == c)
        def _():
            deal(c, *keep)
            deal(1 - c, *send)


OUT_GROUPS = [(0, 0), (0, 1), (1, 0), (1, 1), (2, 0), (3, 0)]


def ff_kernel(
    n_ref, cot_ref, c1_ref, c2_ref, c3_ref,
    bu_ref, bd_ref, g1_ref, s1_ref, g2_ref, s2_ref, wu_ref, wd_ref,
    out_ref, dkeep, dsend, ukeep, usend, dh_ref, dfirst_ref, vsum_ref,
    act, cot, nlow, nlow_t, dd, g_down, g_up,
):
    width = n_ref.shape[1]
    ff = wu_ref.shape[1]
    parts = ff // width
    shares = 2 * dkeep.shape[1]
    unit = width // shares
    span = c1_ref.shape[0]
    me, core = own_blk(), own_core()
    for hop, piece in enumerate((cot_ref[me], c1_ref[...], c2_ref[...], c3_ref[...])):
        cot[block(me ^ hop, span), :] = piece
    normed = n_ref[...] * wide_row(g1_ref) + wide_row(s1_ref)
    nlow[...] = normed.astype(BF)
    nlow_t[...] = nlow[...].T
    for i in range(parts):
        lanes = slice(i * width, (i + 1) * width)
        a, b = gelu_both(nn(nlow[...], wu_ref[:, lanes]) + wide_row(bu_ref)[:, lanes])
        act[:, lanes] = a.astype(BF)
        dh_ref[:, lanes] = b.astype(BF)
    normed = n_ref[...] * wide_row(g1_ref) + wide_row(s1_ref)
    resid = normed + nn(act[...], wd_ref[...]) + wide_row(bd_ref)
    n2, rstd2 = norm_parts(resid)
    out_ref[...] = (n2 * wide_row(g2_ref) + wide_row(s2_ref)).astype(BF)
    c = cot[...].astype(F32)
    vsum_ref[...] = jnp.zeros_like(vsum_ref)
    vsum_ref[GAIN_TWO:GAIN_TWO + 1] = colsum(c * n2)
    vsum_ref[SHIFT_TWO:SHIFT_TWO + 1] = colsum(c)
    d_r2 = norm_back(c * wide_row(g2_ref), n2, rstd2)
    dfirst_ref[...] = d_r2
    dd[...] = d_r2.astype(BF)
    vsum_ref[B_DOWN:B_DOWN + 1] = colsum(dd[...].astype(F32))

    def back(i, carry):
        lanes = block(i, width)
        g_down[...] = tn(act[:, lanes], dd[...]).astype(BF)
        dhc = (nt(dd[...], wd_ref[lanes, :]) * dh_ref[:, lanes].astype(F32)).astype(BF)
        dh_ref[:, lanes] = dhc
        vsum_ref[pl.ds(B_UP + i, 1)] = colsum(dhc.astype(F32))
        g_up[...] = nn(nlow_t[...], dhc).astype(BF)

        def deal(c, down, up):
            for p in range(4):
                at = (c * 4 + p) * unit
                down[p, i] = g_down[at:at + DOWN_Z]
                up[p, i, unit:] = g_down[at + DOWN_Z:at + unit]
            for z in range(shares // 2):
                at = (2 * z + c) * unit
                up[i, z, 0:unit] = g_up[at:at + unit]

        by_core(core, deal, (dkeep, ukeep), (dsend, usend))
        return carry

    lax.fori_loop(0, parts, back, 0)


def mixed_kernel(
    n_ref, rstd_ref, att_ref, dh_ref, dfirst_ref, vin_ref, g1_ref, wu_ref,
    okeep, osend, dr_ref, dd, vsum_ref,
    g_out,
):
    width = n_ref.shape[1]
    shares = 2 * okeep.shape[1]
    unit = width // shares

    def first(i, carry):
        lanes = block(i, width // 3)
        dr_ref[:, lanes] = dfirst_ref[:, lanes] + nt(dh_ref[...], wu_ref[lanes, :])
        return carry

    lax.fori_loop(0, 3, first, 0)
    d_f = dr_ref[...]
    n1 = n_ref[...]
    vsum_ref[...] = vin_ref[...]
    vsum_ref[GAIN_ONE:GAIN_ONE + 1] = colsum(d_f * n1)
    vsum_ref[SHIFT_ONE:SHIFT_ONE + 1] = colsum(d_f)
    d_r1 = norm_back(d_f * wide_row(g1_ref), n1, rstd_ref[:, 0:1])
    dr_ref[...] = d_r1
    db = d_r1.astype(BF)
    dd[...] = db
    vsum_ref[B_OUT:B_OUT + 1] = colsum(db.astype(F32))
    g_out[...] = nn(att_ref[...], dd[...]).astype(BF)

    def deal(c, out):
        for z in range(shares // 2):
            for g in range(unit // GROUP):
                p, at = OUT_GROUPS[g]
                src = (2 * z + c) * unit + g * GROUP
                out[p, z, at * GROUP:(at + 1) * GROUP] = g_out[src:src + GROUP]
            for p in (2, 3):
                out[p, z, GROUP:2 * GROUP] = jnp.zeros((GROUP, width), BF)

    by_core(own_core(), deal, (okeep,), (osend,))


def attended_kernel(att_ref, sum_ref, dd_ref, wo_ref, dst_ref, delta_ref, dm_ref):
    dm_ref[...] = nt(wo_ref[...], dd_ref[...])
    for i in range(HEADS):
        at = slice(i * HD, (i + 1) * HD)
        inv = 1.0 / sum_ref[i]
        delta_ref[i] = colsum(dm_ref[at, :] * att_ref[at, :].astype(F32)) * inv
        dst_ref[at, :] = (dm_ref[at, :] * inv).astype(BF)


def heads_kernel(first, lengths_ref, x_t_ref, vin_ref, q_ref, k_ref, v_ref, dst_ref, delta_ref, max_ref, dq, dk, dv, keep, *sends):
    *sends, g_ref = sends
    length = lengths_ref[own_blk()]
    rows = q_ref.shape[0]
    dead = jnp.where(lax.broadcasted_iota(jnp.int32, (rows, 1), 0) < length, 0.0, NEGATIVE)

    def pair(i, carry):
        lanes, own = block(first + i, 2 * HD), block(i, 2 * HD)
        q2, k2, v2 = q_ref[:, lanes], k_ref[:, lanes], v_ref[:, lanes]
        dst = dst_ref[lanes, :]
        ds2 = dst.T
        k2t = k2.T
        dv2 = jnp.zeros((rows, 2 * HD), F32)
        dk2 = jnp.zeros((rows, 2 * HD), F32)
        dqs = []
        for h in range(2):
            live = head_lanes(q2.shape, h)
            zero = jnp.zeros_like(q2)
            qm = jnp.where(live, q2, zero)
            s = nt(k2, qm) + dead
            head = 2 * (first + i) + h
            p = jnp.exp(s - max_ref[head])
            dp = nn(jnp.where(live, v2, zero), dst)
            dsc = (p * (dp - delta_ref[head])).astype(BF)
            dv2 = dv2 + nn(p.astype(BF), jnp.where(live, ds2, zero))
            dk2 = dk2 + nn(dsc, qm)
            dqs.append(nn(k2t[h * HD:(h + 1) * HD], dsc))
        dq[:, own] = (jnp.concatenate(dqs, axis=0) * SCALE).astype(BF).T
        dk[:, own] = dk2.astype(BF)
        dv[:, own] = dv2.astype(BF)
        return carry

    lax.fori_loop(0, dq.shape[1] // (2 * HD), pair, 0)
    for i, part in enumerate((dq, dk, dv)):
        g_ref[i] = nn(x_t_ref[...], part[...]).astype(BF)
    vsum = vin_ref[:, first * 2 * HD:first * 2 * HD + dq.shape[1]]
    row = lax.broadcasted_iota(jnp.int32, vsum.shape, 0)
    vsum = vsum + jnp.where(row == B_QUERY, colsum(dq[...].astype(F32)), 0.0) + jnp.where(row == B_VALUE, colsum(dv[...].astype(F32)), 0.0)
    high = vsum.astype(BF)
    low = (vsum - high.astype(F32)).astype(BF)
    shares = 2 * keep.shape[1]
    unit = x_t_ref.shape[0] // shares
    tall = keep.shape[2]

    def deal(c, *pieces):
        def one(z, carry):
            for i in range(3):
                for j in range(unit // GROUP):
                    at = i * unit + j * GROUP
                    src = pl.ds(pl.multiple_of((2 * z + c) * unit + j * GROUP, GROUP), GROUP)
                    pieces[at // tall][z, at % tall:at % tall + GROUP] = g_ref[i, src]
            pieces[3][z, tall - 2 * GROUP:tall - GROUP] = high
            pieces[3][z, tall - GROUP:tall] = low
            return carry

        lax.fori_loop(0, shares // 2, one, 0)

    per = 4 // len(sends)
    by_core(own_core(), deal, [keep.at[p] for p in range(4)], [sends[p // per].at[p % per] for p in range(4)])


def inputs_kernel(groups, hit_ref, out_page, dr_ref, wq_ref, wk_ref, wv_ref, *refs):
    parts = [refs[3 * g:3 * g + 3] for g in range(groups)]
    din_ref, *outs = refs[3 * groups:]
    total = dr_ref[...]
    for i, w in enumerate((wq_ref, wk_ref, wv_ref)):
        at = 0
        for part in parts:
            wide = part[i].shape[1]
            total = total + nt(part[i][...], w[:, at:at + wide])
            at += wide
    din_ref[...] = jnp.where(hit_ref[:, 0:1] > 0.5, 0.0, total).astype(BF)
    span = outs[0].shape[1]
    for i, out in enumerate(outs):
        rows = block(own_blk() ^ (i + 1), span)
        out[0] = out_page[rows, :]
        out[1] = din_ref[rows, :]


def added(a, b):
    return (a.astype(F32) + b.astype(F32)).astype(BF)


def halves_kernel(bit, came_parts, own, came, send, keep):
    mine = bit()

    def one(r, carry):
        send[r] = added(own[1 - mine, r], came[1 - mine, r])
        keep[r] = added(own[mine, r], came[mine, r])
        return carry

    lax.fori_loop(0, own.shape[1], one, 0)


def joined_halves_kernel(bit, axis, cuts, *refs):
    owns, rest = refs[:len(cuts)], refs[len(cuts):]
    cames = []
    for n in cuts:
        cames.append(rest[:n])
        rest = rest[n:]
    send, keep = rest
    mine = bit()

    def half_of(half, out, came_half):
        def one(r, carry):
            at = 0
            for own, came in zip(owns, cames):
                size = own.shape[1 + axis]
                cut = slice(at, at + size)
                index = (r, cut) if axis == 1 else (r, slice(None), cut)
                out[index] = added(own[half, r], came[0][half, r] if len(came) == 1 else came[came_half][0, r])
                at += size
            return carry

        lax.fori_loop(0, out.shape[0], one, 0)

    if max(cuts) == 1:
        half_of(1 - mine, send, None)
        half_of(mine, keep, None)
        return
    for half in range(2):

        @pl.when(mine == half)
        def _():
            half_of(1 - half, send, 1 - half)
            half_of(half, keep, half)


def z_halves_kernel(came_parts, own, came, send, keep):
    pieces, depth = own.shape[:2]
    rest = depth // 2
    low, high = z_bits()
    core = own_core()
    if depth == 4:
        mine = jnp.where(core == 0, low, high)
        by_half, by_rest = jnp.where(core == 0, 1, 2), jnp.where(core == 0, 2, 1)
    else:
        mine = jnp.where(core == 0, high, low)
        by_half, by_rest = 1, 0

    def one(j, carry):
        p, r = lax.div(j, rest), lax.rem(j, rest)
        theirs, ours = (1 - mine) * by_half + r * by_rest, mine * by_half + r * by_rest
        send[j] = added(own[p, theirs], came[p, theirs])
        keep[j] = added(own[p, ours], came[p, ours])
        return carry

    lax.fori_loop(0, pieces * rest, one, 0)


def sum_kernel(own, came, out):
    out[...] = added(own[...].reshape(out.shape), came[...].reshape(out.shape))


def pair_kernel(own, came, out):
    lo = second_bit()
    out[lo] = own[...]
    out[1 - lo] = came[...]


def last_kernel(place, own, came, *refs):
    mine = first_bit()
    for half in range(2):
        @pl.when(mine == half)
        def _():
            for j in range(2):
                place(2 * half + j, own, j, *refs)
                place(2 * (1 - half) + j, came, j, *refs)


def place_up(p, ref, j, up, out, tail):
    unit, width = out.shape
    end = unit + tail.shape[1]
    up[:, p * width:(p + 1) * width] = ref[j, 0:unit].astype(F32)
    tail[p] = ref[j, unit:end].astype(F32)
    for g, (piece, at) in enumerate(OUT_GROUPS):
        if piece == p:
            out[g * GROUP:(g + 1) * GROUP] = ref[j, end + at * GROUP:end + (at + 1) * GROUP].astype(F32)


def place_down(p, ref, j, tail, down):
    unit = down.shape[0] // 4
    down[p * unit:p * unit + DOWN_Z] = ref[j].astype(F32)
    down[p * unit + DOWN_Z:(p + 1) * unit] = tail[p]


def place_rows(p, ref, j, query, key, value, vectors):
    unit = query.shape[0]
    tall = ref.shape[1]
    for g in range(tall // GROUP):
        at = p * tall + g * GROUP
        part = ref[j, g * GROUP:(g + 1) * GROUP].astype(F32)
        if at < 3 * unit:
            (query, key, value)[at // unit][at % unit:at % unit + GROUP] = part
        elif at == 3 * unit:
            vectors[...] = part + ref[j, (g + 1) * GROUP:(g + 2) * GROUP].astype(F32)


def page_rows_kernel(out_page, d_page, *refs):
    *came, out_rows, d_rows = refs
    span = out_rows.shape[1]
    me = own_blk()
    for which, (page, out) in enumerate(((out_page, out_rows), (d_page, d_rows))):
        out[me] = page[block(me, span), :]
        for i, part in enumerate(came):
            out[me ^ (i + 1)] = part[which]


VM = pl.BlockSpec(memory_space=pltpu.VMEM)
SM = pl.BlockSpec(memory_space=pltpu.SMEM)
HB = pl.BlockSpec(memory_space=pl.ANY)


def call(kernel, args, places, outs, scratch, limit):
    return pl.pallas_call(
        kernel,
        out_shape=[jax.ShapeDtypeStruct(s, d) for s, d in outs],
        in_specs=places,
        out_specs=[VM] * len(outs),
        scratch_shapes=[s if not isinstance(s, tuple) else pltpu.VMEM(*s) for s in scratch],
        compiler_params=pltpu.CompilerParams(vmem_limit_bytes=limit * MIB),
        cost_estimate=pl.CostEstimate(flops=1024, bytes_accessed=1024, transcendentals=0),
    )(*args)


def fetch(ids, counts, spots, table, rows):
    width = table.shape[1]
    slots = ids.shape[1]
    return call(
        fetch_kernel, (ids, counts, spots, table), [SM, SM, VM, HB], [((rows, width), BF), ((rows, 128), F32)],
        [((slots * GROUP, width), BF), ((slots * GROUP, width), F32), ((slots, width), F32), pltpu.SemaphoreType.DMA], LIMITS[0],
    )


LIMITS = [44, 16, 20, 8, 16, 10, 4]


def attend(lengths, inputs, pieces, placed, hit, biases, wq, wk, wv, wo):
    span, width = pieces[0].shape
    rows = 4 * span
    args = (lengths, inputs, *pieces, placed, hit, *biases, wq, wk, wv, wo)
    outs = [((width, rows), BF)] + [((rows, width), BF)] * 3 + [((width, rows), BF), ((HEADS, 1, rows), F32), ((HEADS, 1, rows), F32), ((rows, width), F32), ((rows, 128), F32)]
    return call(attend_kernel, args, [SM] + [VM] * 13, outs, [((rows, width), BF)] * 2, LIMITS[1])


def feed(n, cotangent, pieces, vecs, wu, wd):
    rows, width = n.shape
    ff = wu.shape[1]
    args = (n, cotangent, *pieces, *vecs, wu, wd)
    unit = width // PARTS
    groups = [((4, PARTS // 2, tall, width), BF) for tall in (DOWN_Z, 2 * unit - DOWN_Z)]
    outs = [((rows, width), BF)] + [groups[0]] * 2 + [groups[1]] * 2 + [((rows, ff), BF), ((rows, width), F32), ((16, width), F32)]
    scratch = [((rows, ff), BF)] + [((rows, width), BF)] * 2 + [((width, rows), BF), ((rows, width), BF)] + [((width, width), BF)] * 2
    return call(ff_kernel, args, [VM] * len(args), outs, scratch, LIMITS[2])


def mixed_back(n, rstd, att, dh, dfirst, vsum, gain, wu):
    rows, width = n.shape
    args = (n, rstd, att, dh, dfirst, vsum, gain, wu)
    group = ((4, PARTS // 2, 2 * GROUP, width), BF)
    outs = [group] * 2 + [((rows, width), F32), ((rows, width), BF), (vsum.shape, F32)]
    return call(mixed_kernel, args, [VM] * len(args), outs, [((width, width), BF)], LIMITS[5])


def attended_back(att, sums, dd, wo):
    rows, width = dd.shape
    outs = [((width, rows), BF), ((HEADS, 1, rows), F32)]
    return call(attended_kernel, (att, sums, dd, wo), [VM] * 4, outs, [((width, rows), F32)], LIMITS[5])


def heads(first, count, cuts, lengths, x_t, vsum, q, k, v, dst, delta, tops):
    width, rows = x_t.shape
    wide = count * HD
    tall = (3 * (width // PARTS) + 2 * GROUP) // 4
    args = (lengths, x_t, vsum, q, k, v, dst, delta, tops)
    outs = [((rows, wide), BF)] * 3 + [((4, PARTS // 2, tall, wide), BF)] + [((4 // cuts, PARTS // 2, tall, wide), BF)] * cuts
    return call(functools.partial(heads_kernel, first // 2), args, [SM] + [VM] * 8, outs, [((3, width, wide), BF)], LIMITS[3])


def inputs_grad(span, hit, out_page, dr, wq, wk, wv, parts):
    rows, width = dr.shape
    args = (hit, out_page, dr, wq, wk, wv) + tuple(t for part in parts for t in part)
    outs = [(dr.shape, BF)] + [((2, span, width), BF)] * (rows // span - 1)
    return call(functools.partial(inputs_kernel, len(parts)), args, [VM] * len(args), outs, [], LIMITS[5])


def pick(array, index, axis=0):
    return lax.dynamic_index_in_dim(array, index, axis, keepdims=False)


def swap(array, bit):
    return lax.ppermute(array, "blk", [(i, i ^ bit) for i in range(lax.axis_size("blk"))])


def swap_first(array, first):
    blks, shares = lax.axis_size("blk"), lax.axis_size("batch")
    perm = []
    for b in range(blks):
        for s in range(shares):
            bit = 1 if (s % 2 == 0) == first else 2
            perm.append((b * shares + s, (b ^ bit) * shares + s))
    return lax.ppermute(array, ("blk", "batch"), perm)


def swap_batch(array, bit):
    return lax.ppermute(array, "batch", [(i, i ^ bit) for i in range(lax.axis_size("batch"))])


def swap_z(array, first):
    shares = lax.axis_size("batch")
    return lax.ppermute(array, "batch", [(i, i ^ (2 if (i % 2 == 0) == first else 4)) for i in range(shares)])


class Cell:
    def __init__(self, *values):
        self.values = values


class Order:
    def __init__(self):
        self.last = Cell()

    def enter(self, *arrays):
        tied = lax.optimization_barrier((*arrays, *self.last.values))
        self.last.values = tied[len(arrays):]
        return tied[:len(arrays)]

    def leave(self, cell):
        self.last = cell


class Chain:
    def __init__(self, order, cell, send):
        self.order = order
        self.own, self.came = cell, tuple(swap_batch(s, 1) for s in send)

    @classmethod
    def joined(cls, order, axis, cells, cames):
        chain = cls(order, None, ())
        groups = len(cells)
        tied = order.enter(*(c.values[0] for c in cells), *(t for came in cames for t in came))
        shape = tied[0].shape
        flat = [shape[0] * shape[1] // 2, shape[2], shape[3]]
        flat[axis] = sum(t.shape[axis + 1] for t in tied[:groups])
        args = [t.reshape((-1, flat[0]) + t.shape[2:]) for t in tied]
        kernel = functools.partial(joined_halves_kernel, first_bit, axis, [len(came) for came in cames])
        send, keep = call(kernel, args, [VM] * len(args), [(tuple(flat), BF)] * 2, [], LIMITS[6])
        chain.came = [swap_first(send, True)]
        chain.own = Cell(keep.reshape((shape[0] // 2, shape[1], flat[1], flat[2])))
        order.leave(chain.own)
        return chain

    def halve(self, axis, bit, move, cuts):
        own, *came = self.order.enter(self.own.values[0], *self.came)
        shape = own.shape
        after = shape[:axis] + (shape[axis] // 2,) + shape[axis + 1:]
        flat = (after[0] * after[1],) + shape[2:]
        if axis == 0:
            own = own.reshape((2,) + flat)
            kernel = functools.partial(halves_kernel, bit, len(came))
        else:
            kernel = functools.partial(z_halves_kernel, len(came))
        came = [came[0].reshape(own.shape)]
        outs = [((flat[0] // cuts,) + shape[2:], BF)] * cuts + [(flat, BF)]
        *sends, keep = call(kernel, (own, *came), [VM] * (1 + len(came)), outs, [], LIMITS[6])
        self.came = [move(send) for send in sends]
        self.own = Cell(keep.reshape(after))
        self.order.leave(self.own)

    def first(self, cuts=1):
        self.halve(0, first_bit, lambda v: swap_first(v, True), cuts)

    def second(self, cuts=1):
        self.halve(0, second_bit, lambda v: swap_first(v, False), cuts)

    def z_first(self, cuts=1):
        self.halve(1, None, lambda v: swap_z(v, True), cuts)

    def z_second(self, cuts=1):
        self.halve(1, None, lambda v: swap_z(v, False), cuts)

    def gather_second(self):
        own, came = self.order.enter(self.own.values[0], *self.came)
        out, = call(sum_kernel, (own, came), [VM] * 2, [(own.shape[2:], BF)], [], LIMITS[6])
        self.own = Cell(out)
        self.came = (swap_first(out, False),)
        self.order.leave(self.own)

    def gather_first(self):
        own, came = self.order.enter(self.own.values[0], *self.came)
        out, = call(pair_kernel, (own, came), [VM] * 2, [((2,) + own.shape, BF)], [], LIMITS[6])
        self.own = Cell(out)
        self.came = (swap_first(out, True),)
        self.order.leave(self.own)

    def result(self, place, shapes, *others):
        own, came = self.order.enter(self.own.values[0], *self.came)
        args = (own, came, *others)
        return call(functools.partial(last_kernel, place), args, [VM] * len(args), [(s, F32) for s in shapes], [], LIMITS[6])


def own_vectors(vec, share, shares):
    width = vec.shape[-1]
    n = width // shares
    cut = lax.dynamic_slice_in_dim(vec, share * n, n, 1)
    flat = vec[B_UP:B_UP + 4].reshape(-1)
    return [cut[i] for i in range(B_UP)] + [lax.dynamic_slice_in_dim(flat, share * 4 * n, 4 * n, 0)]


def body(
    inputs, lengths, positions, counts, token_ids, table,
    w_query, b_query, w_key, w_value, b_value, w_out, b_out, gain_one, shift_one,
    w_up, b_up, w_down, b_down, gain_two, shift_two, cotangent,
):
    blk, share = lax.axis_index("blk"), lax.axis_index("batch")
    shares = lax.axis_size("batch")
    core = share % 2
    pages, span, width = inputs.shape
    ff = w_up.shape[1]
    unit = width // PARTS
    rows_in = [swap(pick(inputs, blk ^ i), i) for i in range(1, pages)]
    placed, hit = fetch(token_ids, counts, positions, table, pages * span)
    back, hit = lax.optimization_barrier((cotangent, hit))
    back_in = [swap(pick(back, blk ^ i), i) for i in range(1, pages)]
    x_t, q, k, v, att, tops, sums, n1, rstd = attend(
        lengths, inputs, rows_in, placed, hit, (b_query, b_value, b_out), w_query, w_key, w_value, w_out
    )
    out_page, d_keep, d_send, u_keep, u_send, dh, dfirst, vsum = feed(
        n1, cotangent, back_in, (b_up, b_down, gain_one, shift_one, gain_two, shift_two), w_up, w_down
    )

    def to_mixed(n1, vsum):
        return mixed_back(n1, rstd, att, dh, dfirst, vsum, gain_one, w_up)

    order = Order()

    def attention_back(first, count, vsum, dst, delta, cuts=1):
        delta, = order.enter(delta)
        dq, dk, dv, keep, *send = heads(first, count, cuts, lengths, x_t, vsum, q, k, v, dst, delta, tops)
        parts = [dq, dk, dv]
        grads = Cell(keep)
        order.leave(grads)
        return parts, grads, send

    def page_rows(out_page, d_page, came):
        return call(page_rows_kernel, (out_page, d_page, *came), [VM] * (pages + 1), [(inputs.shape, BF)] * 2, [], LIMITS[6])

    if shares == PARTS and lax.axis_size("blk") == 4:
        d = Chain(order, Cell(d_keep), [d_send])
        u_came = swap_batch(u_send, 1)
        n_now, = order.enter(n1)
        o_keep, o_send, d_r1, d_branch, vsum = to_mixed(n_now, vsum)
        o_cell = Cell(o_keep)
        order.leave(o_cell)
        o_came = swap_batch(o_send, 1)
        att_now, = order.enter(att)
        sums_cell = Cell(*attended_back(att_now, sums, d_branch, w_out))
        order.leave(sums_cell)
        d.z_first()
        u = Chain.joined(order, 1, [Cell(u_keep), o_cell], [[u_came], [o_came]])
        groups = [attention_back(0, 8, vsum, *sums_cell.values, cuts=2)]
        groups.append(attention_back(8, 4, vsum, *sums_cell.values))
        parts = [g[0] for g in groups]
        a = Chain.joined(order, 2, [g[1] for g in groups], [[swap_batch(t, 1) for t in g[2]] for g in groups])
        d.z_second()
        u.second()
        hit_now, = order.enter(hit)
        d_page, *page_parts = inputs_grad(span, hit_now, out_page, d_r1, w_query, w_key, w_value, parts)
        d_cell = Cell(d_page)
        order.leave(d_cell)
        page_parts = [swap(part, i + 1) for i, part in enumerate(page_parts)]
        a.second()
        u.z_first()
        d.first()
        a.z_first()
        u.z_second()
        d.second()
        a.z_second()
        u.gather_second()
        d.gather_second()
        d_page, *came = order.enter(*d_cell.values, *page_parts)
        rows_cell = Cell(*page_rows(out_page, d_page, came))
        order.leave(rows_cell)
        a.gather_second()
        a.gather_first()
        u.gather_first()
        d.gather_first()
        grad_up, grad_out, tail = u.result(place_up, [(unit, ff), (unit, width), (4, unit - DOWN_Z, width)])
        grad_down, = d.result(place_down, [(ff // PARTS, width)], tail)
        grad_query, grad_key, grad_value, vectors = a.result(place_rows, [(unit, width)] * 3 + [(GROUP, width)])
        outputs, d_inputs = rows_cell.values
    else:
        o_keep, o_send, d_r1, d_branch, vsum = to_mixed(n1, vsum)
        attended = attended_back(att, sums, d_branch, w_out)
        groups = [attention_back(i, 4, vsum, *attended) for i in range(0, HEADS, 4)]
        a_keep = jnp.concatenate([g[1].values[0] for g in groups], axis=-1)
        a_send = jnp.concatenate([g[2][0] for g in groups], axis=-1)
        d_page, *page_parts = inputs_grad(span, hit, out_page, d_r1, w_query, w_key, w_value, [g[0] for g in groups])
        came = [swap(part, i + 1) for i, part in enumerate(page_parts)]
        outputs, d_inputs = page_rows(out_page, d_page, came)

        def parity(keep, send):
            packed = jnp.where(core == 0, jnp.stack([keep, send]), jnp.stack([send, keep]))
            return packed.transpose(1, 2, 0, 3, 4)

        def over(grad):
            part = lax.psum_scatter(grad.astype(F32), "batch", scatter_dimension=0, tiled=True)
            return lax.psum(part.astype(BF), "blk").astype(F32)

        out = parity(o_keep, o_send)
        out = jnp.concatenate([out[p][..., at * GROUP:(at + 1) * GROUP, :] for p, at in OUT_GROUPS], axis=-2)
        out = out.reshape(width, width)
        up = parity(u_keep, u_send)
        down = jnp.concatenate([parity(d_keep, d_send), up[..., unit:, :]], axis=-2)
        down = down.transpose(1, 2, 0, 3, 4).reshape(ff, width)
        up = up[..., :unit, :].transpose(1, 2, 3, 0, 4).reshape(width, ff)
        rows = parity(a_keep, a_send).transpose(1, 2, 0, 3, 4).reshape(PARTS, -1, width)
        mats = [rows[:, i * unit:(i + 1) * unit].reshape(width, width) for i in range(3)]
        vectors = rows[0, 3 * unit:3 * unit + GROUP].astype(F32) + rows[0, 3 * unit + GROUP:].astype(F32)
        vectors = lax.psum(vectors, ("blk", "batch"))
        grad_down, grad_up, grad_out = over(down), over(up), over(out)
        grad_query, grad_key, grad_value = (over(m) for m in mats)
    r = own_vectors(vectors, share, shares)
    return (
        outputs, d_inputs, grad_query, r[B_QUERY], grad_key, grad_value, r[B_VALUE], grad_out, r[B_OUT],
        r[GAIN_ONE], r[SHIFT_ONE], grad_up, r[B_UP], grad_down, r[B_DOWN], r[GAIN_TWO], r[SHIFT_TWO],
    )


def solution(mesh):
    split, whole = P("batch", "blk", None), P()
    rows, vec = P("batch", None), P("batch")
    in_specs = (split, vec, rows, vec, rows) + (whole,) * 16 + (split,)
    out_specs = (split, split, rows, vec, rows, rows, vec, rows, vec, vec, vec, rows, vec, rows, vec, vec, vec)
    return jax.shard_map(body, mesh=mesh, in_specs=in_specs, out_specs=out_specs, check_vma=False)
```

profile of v0, /device:TPU:0, one launch (start us, length us, event | category | flops | bytes accessed | tf_op | source)
XLA Modules:
  0.0 155.5 jit_solution(16196698695125027711)
XLA Ops:
  2.0 3.0 %collective-permute-start = (bf16[128,768]{1,0:T(8,128)(2,1)S(1)}, bf16[128,768]{1,0:T(8,128)(2,1)S(1)}, u32[]{:S(2)}, u32[]{:S(2)}) collective-permute-start(bf16[128,768]{1,0:T(8,128)(2,1)S(1)} %get-tuple-element.332), channel_id=1, source_target_pairs={{0,8},{8,0},{16,24},{24,16},{1,9},{9,1},{17,25},{25,17},{2,10},{10... | collective-permute-start | bytes 589832 | tf_op jit(solution)/shard_map/ppermute | solution.py:580
  5.0 1.5 collective-permute-start.1
  8.9 3.8 %shard_map.341 = (bf16[512,768]{1,0:T(8,128)(2,1)S(1)}, f32[512,128]{1,0:T(8,128)S(1)}) custom-call(s32[4,80]{1,0:T(4,128)S(1)} %copy-done.9, s32[4]{0:T(128)S(1)} %copy-done.18, s32[4,80]{1,0:T(4,128)S(1)} %copy-done.10, bf16[15360,768]{1,0:T(8,128)(2,1)} %table_ref.1), custom_call_target="tpu_custom_call" | custom-call | flops 1024 | bytes 1024 | tf_op jit(solution)/shard_map/pallas_call | solution.py:503
  12.7 1.9 %collective-permute-start.3 = (bf16[128,768]{1,0:T(8,128)(2,1)S(1)}, bf16[128,768]{1,0:T(8,128)(2,1)S(1)}, u32[]{:S(2)}, u32[]{:S(2)}) collective-permute-start(bf16[128,768]{1,0:T(8,128)(2,1)S(1)} %get-tuple-element.329), channel_id=1, source_target_pairs={{0,8},{8,0},{16,24},{24,16},{1,9},{9,1},{17,25},{25,17},{2,10},{10... | collective-permute-start | bytes 589832 | tf_op jit(solution)/shard_map/ppermute | solution.py:580
  14.6 1.5 collective-permute-start.4
  16.4 9.4 %shard_map.342 = (bf16[768,512]{1,0:T(8,128)(2,1)S(1)}, bf16[512,768]{1,0:T(8,128)(2,1)S(1)}, bf16[512,768]{1,0:T(8,128)(2,1)S(1)}, bf16[512,768]{1,0:T(8,128)(2...) custom-call(s32[4]{0:T(128)S(1)} %copy-done.8, ...), custom_call_target="tpu_custom_call" | custom-call | flops 1024 | bytes 1024 | tf_op jit(solution)/shard_map/pallas_call | solution.py:503
  26.0 19.5 %shard_map.343 = (bf16[512,768]{1,0:T(8,128)(2,1)S(1)}, bf16[4,4,80,768]{3,2,1,0:T(8,128)(2,1)S(1)}, bf16[4,4,80,768]{3,2,1,0:T(8,128)(2,1)S(1)}, bf16[4,4,112,7...) custom-call(f32[512,768]{1,0:T(8,128)S(1)} %get-tuple-element.175.n_, ...), custom_call_target="tpu_custom_call" | custom-call | flops 1024 | bytes 1024 | tf_op jit(solution)/shard_map/pallas_call | solution.py:503
  46.1 5.0 %shard_map.344 = (bf16[4,4,32,768]{3,2,1,0:T(8,128)(2,1)S(1)}, bf16[4,4,32,768]{3,2,1,0:T(8,128)(2,1)S(1)}, f32[512,768]{1,0:T(8,128)S(1)}, bf16[512,768]{1,0:T(8,128)(2,1)S(1)}, f32[16,768]{1,0:T(8,128)S(1)}) custom-call(f32[512,768]{1,0:T(8,128)S(1)} %get-tuple-element.175.n_ref, f32[512,128]{1,0:T(8,128)S(1)} %get-tuple-element.180.rstd_ref, ...), custom_call_target="tpu_custom_call" | custom-call | flops 1024 | bytes 1024 | tf_op jit(solution)/shard_map/pallas_call | solution.py:503
  55.5 1.9 %collective-permute-start.9 = (bf16[8,144,768]{2,1,0:T(8,128)(2,1)S(1)}, bf16[8,144,768]{2,1,0:T(8,128)(2,1)S(1)}, u32[]{:S(2)}, u32[]{:S(2)}) collective-permute-start(bf16[8,144,768]{2,1,0:T(8,128)(2,1)S(1)} %get-tuple-element.204), channel_id=1, source_target_pairs={{0,8},{1,17},{2,10},{3,19},{4,12},{5,21},{6,14},{7,23},{8,0},{9,25... | collective-permute-start | bytes 5308424 | tf_op jit(solution)/shard_map/ppermute | solution.py:590
  57.4 1.6 %collective-permute-start.10 = (bf16[8,80,768]{2,1,0:T(8,128)(2,1)S(1)}, bf16[8,80,768]{2,1,0:T(8,128)(2,1)S(1)}, u32[]{:S(2)}, u32[]{:S(2)}) collective-permute-start(bf16[8,80,768]{2,1,0:T(8,128)(2,1)S(1)} %get-tuple-element.206), channel_id=1, source_target_pairs={{0,2},{1,5},{2,0},{3,7},{4,6},{5,1},{6,4},{7,3},{8,10},{9,13},{10,... | collective-permute-start | bytes 2949128 | tf_op jit(solution)/shard_map/ppermute | solution.py:599
  58.9 8.8 %shard_map.348 = (bf16[512,512]{1,0:T(8,128)(2,1)S(1)}, bf16[512,512]{1,0:T(8,128)(2,1)S(1)}, bf16[512,512]{1,0:T(8,128)(2,1)S(1)}, bf16[4,4,80,512]{3,2,1,0:T(8...) custom-call(s32[4]{0:T(128)S(1)} %copy-done.8, ...), custom_call_target="tpu_custom_call" | custom-call | flops 1024 | bytes 1024 | tf_op jit(solution)/shard_map/pallas_call | solution.py:503
  67.7 4.8 %shard_map.349 = (bf16[512,256]{1,0:T(8,128)(2,1)S(1)}, bf16[512,256]{1,0:T(8,128)(2,1)S(1)}, bf16[512,256]{1,0:T(8,128)(2,1)S(1)}, bf16[4,4,80,256]{3,2,1,0:T(8,128)(2,1)S(1)}, bf16[4,4,80,256]{3,2,1,0:T(8,128)(2,1)S(1)}) custom-call(s32[4]{0:T(128)S(1)} %copy-done.8, bf16[768,512]{1,0:T(8,128)(2,1)S(1)} %get-tuple-element.207.x_t_ref, ...), custom_call_target="tpu_custom_call" | custom-call | flops 1024 | bytes 1024 | tf_op jit(solution)/shard_map/pallas_call | solution.py:503
  77.3 1.5 collective-permute-start.15
  78.8 2.8 %collective-permute-done.10 = bf16[8,80,768]{2,1,0:T(8,128)(2,1)S(1)} collective-permute-done((bf16[8,80,768]{2,1,0:T(8,128)(2,1)S(1)}, bf16[8,80,768]{2,1,0:T(8,128)(2,1)S(1)}, u32[]{:S(2)}, u32[]{:S(2)}) %collective-permute-start.10) | collective-permute-done | bytes 983072 | tf_op jit(solution)/shard_map/ppermute | solution.py:599
  82.5 3.3 %collective-permute-start.17 = (bf16[4,80,768]{2,1,0:T(8,128)(2,1)S(1)}, bf16[4,80,768]{2,1,0:T(8,128)(2,1)S(1)}, u32[]{:S(2)}, u32[]{:S(2)}) collective-permute-start(bf16[4,80,768]{2,1,0:T(8,128)(2,1)S(1)} %get-tuple-element.254), channel_id=1, source_target_pairs={{0,4},{1,3},{2,6},{3,1},{4,0},{5,7},{6,2},{7,5},{8,12},{9,11},{10,... | collective-permute-start | bytes 1474568 | tf_op jit(solution)/shard_map/ppermute | solution.py:599
  85.8 2.1 %shard_map.353 = (bf16[512,768]{1,0:T(8,128)(2,1)S(1)}, bf16[2,128,768]{2,1,0:T(8,128)(2,1)S(1)}, bf16[2,128,768]{2,1,0:T(8,128)(2,1)S(1)}, bf16[2,128,768]{2,1,0:T(8,128)(2,1)S(1)}) custom-call(f32[512,128]{1,0:T(8,128)S(1)} %get-tuple-element.238.hit_ref, bf16[512,768]{1,0:T(8,128)(2,1)S(1)} %get-tuple-element.239.out_page, ...), custom_call_target="tpu_custom_call" | custom-call | flops 1024 | bytes 1024 | tf_op jit(solution)/shard_map/pallas_call | solution.py:503
  88.0 9.9 %collective-permute-done.15 = bf16[8,80,768]{2,1,0:T(8,128)(2,1)S(1)} collective-permute-done((bf16[8,80,768]{2,1,0:T(8,128)(2,1)S(1)}, bf16[8,80,768]{2,1,0:T(8,128)(2,1)S(1)}, u32[]{:S(2)}, u32[]{:S(2)}) %collective-permute-start.15) | collective-permute-done | bytes 983072 | tf_op jit(solution)/shard_map/ppermute | solution.py:590
  98.1 1.9 %collective-permute-start.16 = (bf16[4,80,768]{2,1,0:T(8,128)(2,1)S(1)}, bf16[4,80,768]{2,1,0:T(8,128)(2,1)S(1)}, u32[]{:S(2)}, u32[]{:S(2)}) collective-permute-start(bf16[4,80,768]{2,1,0:T(8,128)(2,1)S(1)} %get-tuple-element.252), channel_id=1, source_target_pairs={{0,16},{1,9},{2,18},{3,11},{4,20},{5,13},{6,22},{7,15},{8,24},{9,1... | collective-permute-start | bytes 1474568 | tf_op jit(solution)/shard_map/ppermute | solution.py:590
  100.6 1.6 %collective-permute-start.19 = (bf16[2,144,768]{2,1,0:T(8,128)(2,1)S(1)}, bf16[2,144,768]{2,1,0:T(8,128)(2,1)S(1)}, u32[]{:S(2)}, u32[]{:S(2)}) collective-permute-start(bf16[2,144,768]{2,1,0:T(8,128)(2,1)S(1)} %get-tuple-element.264), channel_id=1, source_target_pairs={{0,2},{1,5},{2,0},{3,7},{4,6},{5,1},{6,4},{7,3},{8,10},{9,13},{10,... | collective-permute-start | bytes 1327112 | tf_op jit(solution)/shard_map/ppermute | solution.py:599
  102.3 1.5 collective-permute-start.18
  103.9 4.1 %collective-permute-done.16 = bf16[4,80,768]{2,1,0:T(8,128)(2,1)S(1)} collective-permute-done((bf16[4,80,768]{2,1,0:T(8,128)(2,1)S(1)}, bf16[4,80,768]{2,1,0:T(8,128)(2,1)S(1)}, u32[]{:S(2)}, u32[]{:S(2)}) %collective-permute-start.16) | collective-permute-done | bytes 491552 | tf_op jit(solution)/shard_map/ppermute | solution.py:590
  108.1 3.7 %collective-permute-start.21 = (bf16[2,80,768]{2,1,0:T(8,128)(2,1)S(1)}, bf16[2,80,768]{2,1,0:T(8,128)(2,1)S(1)}, u32[]{:S(2)}, u32[]{:S(2)}) collective-permute-start(bf16[2,80,768]{2,1,0:T(8,128)(2,1)S(1)} %get-tuple-element.274), channel_id=1, source_target_pairs={{0,2},{1,5},{2,0},{3,7},{4,6},{5,1},{6,4},{7,3},{8,10},{9,13},{10,... | collective-permute-start | bytes 737288 | tf_op jit(solution)/shard_map/ppermute | solution.py:599
  113.8 1.6 %collective-permute-start.25 = (bf16[2,128,768]{2,1,0:T(8,128)(2,1)S(1)}, bf16[2,128,768]{2,1,0:T(8,128)(2,1)S(1)}, u32[]{:S(2)}, u32[]{:S(2)}) collective-permute-start(bf16[2,128,768]{2,1,0:T(8,128)(2,1)S(1)} %get-tuple-element.286), channel_id=1, source_target_pairs={{0,24},{8,16},{16,8},{24,0},{1,25},{9,17},{17,9},{25,1},{2,26},{10... | collective-permute-start | bytes 1179656 | tf_op jit(solution)/shard_map/ppermute | solution.py:580
  115.5 1.9 %collective-permute-start.20 = (bf16[1,144,768]{2,1,0:T(8,128)(2,1)S(1)}, bf16[1,144,768]{2,1,0:T(8,128)(2,1)S(1)}, u32[]{:S(2)}, u32[]{:S(2)}) collective-permute-start(bf16[1,144,768]{2,1,0:T(8,128)(2,1)S(1)} %get-tuple-element.272), channel_id=1, source_target_pairs={{0,4},{1,3},{2,6},{3,1},{4,0},{5,7},{6,2},{7,5},{8,12},{9,11},{10,... | collective-permute-start | bytes 663560 | tf_op jit(solution)/shard_map/ppermute | solution.py:599
  117.5 2.1 %collective-permute-done.21 = bf16[2,80,768]{2,1,0:T(8,128)(2,1)S(1)} collective-permute-done((bf16[2,80,768]{2,1,0:T(8,128)(2,1)S(1)}, bf16[2,80,768]{2,1,0:T(8,128)(2,1)S(1)}, u32[]{:S(2)}, u32[]{:S(2)}) %collective-permute-start.21) | collective-permute-done | bytes 245792 | tf_op jit(solution)/shard_map/ppermute | solution.py:599
  119.7 4.2 %collective-permute-done.20.came = bf16[1,144,768]{2,1,0:T(8,128)(2,1)S(1)} collective-permute-done((bf16[1,144,768]{2,1,0:T(8,128)(2,1)S(1)}, bf16[1,144,768]{2,1,0:T(8,128)(2,1)S(1)}, u32[]{:S(2)}, u32[]{:S(2)}) %collective-permute-start.20) | collective-permute-done | bytes 221216 | tf_op jit(solution)/shard_map/ppermute | solution.py:599
  123.8 2.4 %collective-permute-start.22 = (bf16[1,80,768]{2,1,0:T(8,128)(2,1)S(1)}, bf16[1,80,768]{2,1,0:T(8,128)(2,1)S(1)}, u32[]{:S(2)}, u32[]{:S(2)}) collective-permute-start(bf16[1,80,768]{2,1,0:T(8,128)(2,1)S(1)} %get-tuple-element.282), channel_id=1, source_target_pairs={{0,4},{1,3},{2,6},{3,1},{4,0},{5,7},{6,2},{7,5},{8,12},{9,11},{10,... | collective-permute-start | bytes 368648 | tf_op jit(solution)/shard_map/ppermute | solution.py:599
  126.3 5.0 %collective-permute-done.26.came = bf16[1,80,768]{2,1,0:T(8,128)(2,1)S(1)} collective-permute-done((bf16[1,80,768]{2,1,0:T(8,128)(2,1)S(1)}, bf16[1,80,768]{2,1,0:T(8,128)(2,1)S(1)}, u32[]{:S(2)}, u32[]{:S(2)}) %collective-permute-start.26) | collective-permute-done | bytes 122912 | tf_op jit(solution)/shard_map/ppermute | solution.py:590
  134.7 4.2 %collective-permute-done.28.came = bf16[80,768]{1,0:T(8,128)(2,1)S(1)} collective-permute-done((bf16[80,768]{1,0:T(8,128)(2,1)S(1)}, bf16[80,768]{1,0:T(8,128)(2,1)S(1)}, u32[]{:S(2)}, u32[]{:S(2)}) %collective-permute-start.28) | collective-permute-done | bytes 122912 | tf_op jit(solution)/shard_map/ppermute | solution.py:590
  139.1 1.6 %collective-permute-start.31 = (bf16[2,144,768]{2,1,0:T(8,128)(2,1)S(1)}, bf16[2,144,768]{2,1,0:T(8,128)(2,1)S(1)}, u32[]{:S(2)}, u32[]{:S(2)}) collective-permute-start(bf16[2,144,768]{2,1,0:T(8,128)(2,1)S(1)} %shard_map.367.own), channel_id=1, source_target_pairs={{0,8},{1,17},{2,10},{3,19},{4,12},{5,21},{6,14},{7,23},{8,0},{9,25... | collective-permute-start | bytes 1327112 | tf_op jit(solution)/shard_map/ppermute | solution.py:590
  142.1 4.8 %collective-permute-done.30.came = bf16[80,768]{1,0:T(8,128)(2,1)S(1)} collective-permute-done((bf16[80,768]{1,0:T(8,128)(2,1)S(1)}, bf16[80,768]{1,0:T(8,128)(2,1)S(1)}, u32[]{:S(2)}, u32[]{:S(2)}) %collective-permute-start.30) | collective-permute-done | bytes 122912 | tf_op jit(solution)/shard_map/ppermute | solution.py:590
  147.5 2.5 %collective-permute-done.29.came = bf16[2,80,768]{2,1,0:T(8,128)(2,1)S(1)} collective-permute-done((bf16[2,80,768]{2,1,0:T(8,128)(2,1)S(1)}, bf16[2,80,768]{2,1,0:T(8,128)(2,1)S(1)}, u32[]{:S(2)}, u32[]{:S(2)}) %collective-permute-start.29) | collective-permute-done | bytes 245792 | tf_op jit(solution)/shard_map/ppermute | solution.py:590
  (118 shorter events, 28.8 us)
Async XLA Ops:
  2.0 14.1 %collective-permute-start = (bf16[128,768]{1,0:T(8,128)(2,1)S(1)}, bf16[128,768]{1,0:T(8,128)(2,1)S(1)}, u32[]{:S(2)}, u32[]{:S(2)}) collective-permute-start(bf16[128,768]{1,0:T(8,128)(2,1)S(1)} %get-tuple-element.332), channel_id=1, source_target_pairs={{0,8},{8,0},{16,24},{24,16},{1,9},{9,1},{17,25},{25,17},{2,10},{10... | collective-permute-start | bytes 589832 | tf_op jit(solution)/shard_map/ppermute | solution.py:580
  5.0 11.2 %collective-permute-start.1 = (bf16[128,768]{1,0:T(8,128)(2,1)S(1)}, bf16[128,768]{1,0:T(8,128)(2,1)S(1)}, u32[]{:S(2)}, u32[]{:S(2)}) collective-permute-start(bf16[128,768]{1,0:T(8,128)(2,1)S(1)} %get-tuple-element.331), channel_id=1, source_target_pairs={{0,16},{8,24},{16,0},{24,8},{1,17},{9,25},{17,1},{25,9},{2,18},{10... | collective-permute-start | bytes 589832 | tf_op jit(solution)/shard_map/ppermute | solution.py:580
  6.6 9.7 %collective-permute-start.2 = (bf16[128,768]{1,0:T(8,128)(2,1)S(1)}, bf16[128,768]{1,0:T(8,128)(2,1)S(1)}, u32[]{:S(2)}, u32[]{:S(2)}) collective-permute-start(bf16[128,768]{1,0:T(8,128)(2,1)S(1)} %get-tuple-element.330), channel_id=1, source_target_pairs={{0,24},{8,16},{16,8},{24,0},{1,25},{9,17},{17,9},{25,1},{2,26},{10... | collective-permute-start | bytes 589832 | tf_op jit(solution)/shard_map/ppermute | solution.py:580
  12.7 13.2 %collective-permute-start.3 = (bf16[128,768]{1,0:T(8,128)(2,1)S(1)}, bf16[128,768]{1,0:T(8,128)(2,1)S(1)}, u32[]{:S(2)}, u32[]{:S(2)}) collective-permute-start(bf16[128,768]{1,0:T(8,128)(2,1)S(1)} %get-tuple-element.329), channel_id=1, source_target_pairs={{0,8},{8,0},{16,24},{24,16},{1,9},{9,1},{17,25},{25,17},{2,10},{10... | collective-permute-start | bytes 589832 | tf_op jit(solution)/shard_map/ppermute | solution.py:580
  14.6 11.3 %collective-permute-start.4 = (bf16[128,768]{1,0:T(8,128)(2,1)S(1)}, bf16[128,768]{1,0:T(8,128)(2,1)S(1)}, u32[]{:S(2)}, u32[]{:S(2)}) collective-permute-start(bf16[128,768]{1,0:T(8,128)(2,1)S(1)} %get-tuple-element.328), channel_id=1, source_target_pairs={{0,16},{8,24},{16,0},{24,8},{1,17},{9,25},{17,1},{25,9},{2,18},{10... | collective-permute-start | bytes 589832 | tf_op jit(solution)/shard_map/ppermute | solution.py:580
  16.1 9.8 %collective-permute-start.5 = (bf16[128,768]{1,0:T(8,128)(2,1)S(1)}, bf16[128,768]{1,0:T(8,128)(2,1)S(1)}, u32[]{:S(2)}, u32[]{:S(2)}) collective-permute-start(bf16[128,768]{1,0:T(8,128)(2,1)S(1)} %get-tuple-element.327), channel_id=1, source_target_pairs={{0,24},{8,16},{16,8},{24,0},{1,25},{9,17},{17,9},{25,1},{2,26},{10... | collective-permute-start | bytes 589832 | tf_op jit(solution)/shard_map/ppermute | solution.py:580
  45.5 9.1 %collective-permute-start.7 = (bf16[4,4,112,768]{3,2,1,0:T(8,128)(2,1)S(1)}, bf16[4,4,112,768]{3,2,1,0:T(8,128)(2,1)S(1)}, u32[]{:S(2)}, u32[]{:S(2)}) collective-permute-start(bf16[4,4,112,768]{3,2,1,0:T(8,128)(2,1)S(1)} %get-tuple-element.193), channel_id=1, source_target_pairs={{0,1},{1,0},{2,3},{3,2},{4,5},{5,4},{6,7},{7,6},{8,9},{9,8},{10,11... | collective-permute-start | bytes 8257544 | tf_op jit(solution)/shard_map/ppermute | solution.py:594
  45.6 7.9 %collective-permute-start.6 = (bf16[4,4,80,768]{3,2,1,0:T(8,128)(2,1)S(1)}, bf16[4,4,80,768]{3,2,1,0:T(8,128)(2,1)S(1)}, u32[]{:S(2)}, u32[]{:S(2)}) collective-permute-start(bf16[4,4,80,768]{3,2,1,0:T(8,128)(2,1)S(1)} %get-tuple-element.178), channel_id=1, source_target_pairs={{0,1},{1,0},{2,3},{3,2},{4,5},{5,4},{6,7},{7,6},{8,9},{9,8},{10,11... | collective-permute-start | bytes 5898248 | tf_op jit(solution)/shard_map/ppermute | solution.py:594
  51.1 3.5 %collective-permute-start.8 = (bf16[4,4,32,768]{3,2,1,0:T(8,128)(2,1)S(1)}, bf16[4,4,32,768]{3,2,1,0:T(8,128)(2,1)S(1)}, u32[]{:S(2)}, u32[]{:S(2)}) collective-permute-start(bf16[4,4,32,768]{3,2,1,0:T(8,128)(2,1)S(1)} %get-tuple-element.194), channel_id=1, source_target_pairs={{0,1},{1,0},{2,3},{3,2},{4,5},{5,4},{6,7},{7,6},{8,9},{9,8},{10,11... | collective-permute-start | bytes 2359304 | tf_op jit(solution)/shard_map/ppermute | solution.py:594
  55.5 26.4 %collective-permute-start.9 = (bf16[8,144,768]{2,1,0:T(8,128)(2,1)S(1)}, bf16[8,144,768]{2,1,0:T(8,128)(2,1)S(1)}, u32[]{:S(2)}, u32[]{:S(2)}) collective-permute-start(bf16[8,144,768]{2,1,0:T(8,128)(2,1)S(1)} %get-tuple-element.204), channel_id=1, source_target_pairs={{0,8},{1,17},{2,10},{3,19},{4,12},{5,21},{6,14},{7,23},{8,0},{9,25... | collective-permute-start | bytes 5308424 | tf_op jit(solution)/shard_map/ppermute | solution.py:590
  57.4 24.3 %collective-permute-start.10 = (bf16[8,80,768]{2,1,0:T(8,128)(2,1)S(1)}, bf16[8,80,768]{2,1,0:T(8,128)(2,1)S(1)}, u32[]{:S(2)}, u32[]{:S(2)}) collective-permute-start(bf16[8,80,768]{2,1,0:T(8,128)(2,1)S(1)} %get-tuple-element.206), channel_id=1, source_target_pairs={{0,2},{1,5},{2,0},{3,7},{4,6},{5,1},{6,4},{7,3},{8,10},{9,13},{10,... | collective-permute-start | bytes 2949128 | tf_op jit(solution)/shard_map/ppermute | solution.py:599
  73.2 2.7 %collective-permute-start.11 = (bf16[2,4,80,512]{3,2,1,0:T(8,128)(2,1)S(1)}, bf16[2,4,80,512]{3,2,1,0:T(8,128)(2,1)S(1)}, u32[]{:S(2)}, u32[]{:S(2)}) collective-permute-start(bf16[2,4,80,512]{3,2,1,0:T(8,128)(2,1)S(1)} %get-tuple-element.219), channel_id=1, source_target_pairs={{0,1},{1,0},{2,3},{3,2},{4,5},{5,4},{6,7},{7,6},{8,9},{9,8},{10,11... | collective-permute-start | bytes 1966088 | tf_op jit(solution)/shard_map/ppermute | solution.py:594
  73.2 3.5 %collective-permute-start.12 = (bf16[2,4,80,512]{3,2,1,0:T(8,128)(2,1)S(1)}, bf16[2,4,80,512]{3,2,1,0:T(8,128)(2,1)S(1)}, u32[]{:S(2)}, u32[]{:S(2)}) collective-permute-start(bf16[2,4,80,512]{3,2,1,0:T(8,128)(2,1)S(1)} %get-tuple-element.220), channel_id=1, source_target_pairs={{0,1},{1,0},{2,3},{3,2},{4,5},{5,4},{6,7},{7,6},{8,9},{9,8},{10,11... | collective-permute-start | bytes 1966088 | tf_op jit(solution)/shard_map/ppermute | solution.py:594
  77.3 20.6 %collective-permute-start.15 = (bf16[8,80,768]{2,1,0:T(8,128)(2,1)S(1)}, bf16[8,80,768]{2,1,0:T(8,128)(2,1)S(1)}, u32[]{:S(2)}, u32[]{:S(2)}) collective-permute-start(bf16[8,80,768]{2,1,0:T(8,128)(2,1)S(1)} %get-tuple-element.237), channel_id=1, source_target_pairs={{0,8},{1,17},{2,10},{3,19},{4,12},{5,21},{6,14},{7,23},{8,0},{9,25... | collective-permute-start | bytes 2949128 | tf_op jit(solution)/shard_map/ppermute | solution.py:590
  82.4 18.0 %collective-permute-start.14 = (bf16[4,144,768]{2,1,0:T(8,128)(2,1)S(1)}, bf16[4,144,768]{2,1,0:T(8,128)(2,1)S(1)}, u32[]{:S(2)}, u32[]{:S(2)}) collective-permute-start(bf16[4,144,768]{2,1,0:T(8,128)(2,1)S(1)} %get-tuple-element.235), channel_id=1, source_target_pairs={{0,16},{1,9},{2,18},{3,11},{4,20},{5,13},{6,22},{7,15},{8,24},{9,1... | collective-permute-start | bytes 2654216 | tf_op jit(solution)/shard_map/ppermute | solution.py:590
  82.5 19.7 %collective-permute-start.17 = (bf16[4,80,768]{2,1,0:T(8,128)(2,1)S(1)}, bf16[4,80,768]{2,1,0:T(8,128)(2,1)S(1)}, u32[]{:S(2)}, u32[]{:S(2)}) collective-permute-start(bf16[4,80,768]{2,1,0:T(8,128)(2,1)S(1)} %get-tuple-element.254), channel_id=1, source_target_pairs={{0,4},{1,3},{2,6},{3,1},{4,0},{5,7},{6,2},{7,5},{8,12},{9,11},{10,... | collective-permute-start | bytes 1474568 | tf_op jit(solution)/shard_map/ppermute | solution.py:599
  98.1 9.9 %collective-permute-start.16 = (bf16[4,80,768]{2,1,0:T(8,128)(2,1)S(1)}, bf16[4,80,768]{2,1,0:T(8,128)(2,1)S(1)}, u32[]{:S(2)}, u32[]{:S(2)}) collective-permute-start(bf16[4,80,768]{2,1,0:T(8,128)(2,1)S(1)} %get-tuple-element.252), channel_id=1, source_target_pairs={{0,16},{1,9},{2,18},{3,11},{4,20},{5,13},{6,22},{7,15},{8,24},{9,1... | collective-permute-start | bytes 1474568 | tf_op jit(solution)/shard_map/ppermute | solution.py:590
  100.6 13.3 %collective-permute-start.19 = (bf16[2,144,768]{2,1,0:T(8,128)(2,1)S(1)}, bf16[2,144,768]{2,1,0:T(8,128)(2,1)S(1)}, u32[]{:S(2)}, u32[]{:S(2)}) collective-permute-start(bf16[2,144,768]{2,1,0:T(8,128)(2,1)S(1)} %get-tuple-element.264), channel_id=1, source_target_pairs={{0,2},{1,5},{2,0},{3,7},{4,6},{5,1},{6,4},{7,3},{8,10},{9,13},{10,... | collective-permute-start | bytes 1327112 | tf_op jit(solution)/shard_map/ppermute | solution.py:599
  102.3 13.2 %collective-permute-start.18 = (bf16[2,80,768]{2,1,0:T(8,128)(2,1)S(1)}, bf16[2,80,768]{2,1,0:T(8,128)(2,1)S(1)}, u32[]{:S(2)}, u32[]{:S(2)}) collective-permute-start(bf16[2,80,768]{2,1,0:T(8,128)(2,1)S(1)} %get-tuple-element.262), channel_id=1, source_target_pairs={{0,8},{1,17},{2,10},{3,19},{4,12},{5,21},{6,14},{7,23},{8,0},{9,25... | collective-permute-start | bytes 737288 | tf_op jit(solution)/shard_map/ppermute | solution.py:590
  108.1 11.4 %collective-permute-start.21 = (bf16[2,80,768]{2,1,0:T(8,128)(2,1)S(1)}, bf16[2,80,768]{2,1,0:T(8,128)(2,1)S(1)}, u32[]{:S(2)}, u32[]{:S(2)}) collective-permute-start(bf16[2,80,768]{2,1,0:T(8,128)(2,1)S(1)} %get-tuple-element.274), channel_id=1, source_target_pairs={{0,2},{1,5},{2,0},{3,7},{4,6},{5,1},{6,4},{7,3},{8,10},{9,13},{10,... | collective-permute-start | bytes 737288 | tf_op jit(solution)/shard_map/ppermute | solution.py:599
  111.9 20.8 %collective-permute-start.23 = (bf16[2,128,768]{2,1,0:T(8,128)(2,1)S(1)}, bf16[2,128,768]{2,1,0:T(8,128)(2,1)S(1)}, u32[]{:S(2)}, u32[]{:S(2)}) collective-permute-start(bf16[2,128,768]{2,1,0:T(8,128)(2,1)S(1)} %get-tuple-element.284), channel_id=1, source_target_pairs={{0,8},{8,0},{16,24},{24,16},{1,9},{9,1},{17,25},{25,17},{2,10},{10... | collective-permute-start | bytes 1179656 | tf_op jit(solution)/shard_map/ppermute | solution.py:580
  113.3 19.4 %collective-permute-start.24 = (bf16[2,128,768]{2,1,0:T(8,128)(2,1)S(1)}, bf16[2,128,768]{2,1,0:T(8,128)(2,1)S(1)}, u32[]{:S(2)}, u32[]{:S(2)}) collective-permute-start(bf16[2,128,768]{2,1,0:T(8,128)(2,1)S(1)} %get-tuple-element.285), channel_id=1, source_target_pairs={{0,16},{8,24},{16,0},{24,8},{1,17},{9,25},{17,1},{25,9},{2,18},{10... | collective-permute-start | bytes 1179656 | tf_op jit(solution)/shard_map/ppermute | solution.py:580
  113.8 18.9 %collective-permute-start.25 = (bf16[2,128,768]{2,1,0:T(8,128)(2,1)S(1)}, bf16[2,128,768]{2,1,0:T(8,128)(2,1)S(1)}, u32[]{:S(2)}, u32[]{:S(2)}) collective-permute-start(bf16[2,128,768]{2,1,0:T(8,128)(2,1)S(1)} %get-tuple-element.286), channel_id=1, source_target_pairs={{0,24},{8,16},{16,8},{24,0},{1,25},{9,17},{17,9},{25,1},{2,26},{10... | collective-permute-start | bytes 1179656 | tf_op jit(solution)/shard_map/ppermute | solution.py:580
  115.5 8.3 %collective-permute-start.20 = (bf16[1,144,768]{2,1,0:T(8,128)(2,1)S(1)}, bf16[1,144,768]{2,1,0:T(8,128)(2,1)S(1)}, u32[]{:S(2)}, u32[]{:S(2)}) collective-permute-start(bf16[1,144,768]{2,1,0:T(8,128)(2,1)S(1)} %get-tuple-element.272), channel_id=1, source_target_pairs={{0,4},{1,3},{2,6},{3,1},{4,0},{5,7},{6,2},{7,5},{8,12},{9,11},{10,... | collective-permute-start | bytes 663560 | tf_op jit(solution)/shard_map/ppermute | solution.py:599
  119.6 11.7 %collective-permute-start.26 = (bf16[1,80,768]{2,1,0:T(8,128)(2,1)S(1)}, bf16[1,80,768]{2,1,0:T(8,128)(2,1)S(1)}, u32[]{:S(2)}, u32[]{:S(2)}) collective-permute-start(bf16[1,80,768]{2,1,0:T(8,128)(2,1)S(1)} %get-tuple-element.288), channel_id=1, source_target_pairs={{0,16},{1,9},{2,18},{3,11},{4,20},{5,13},{6,22},{7,15},{8,24},{9,1... | collective-permute-start | bytes 368648 | tf_op jit(solution)/shard_map/ppermute | solution.py:590
  123.8 10.1 %collective-permute-start.22 = (bf16[1,80,768]{2,1,0:T(8,128)(2,1)S(1)}, bf16[1,80,768]{2,1,0:T(8,128)(2,1)S(1)}, u32[]{:S(2)}, u32[]{:S(2)}) collective-permute-start(bf16[1,80,768]{2,1,0:T(8,128)(2,1)S(1)} %get-tuple-element.282), channel_id=1, source_target_pairs={{0,4},{1,3},{2,6},{3,1},{4,0},{5,7},{6,2},{7,5},{8,12},{9,11},{10,... | collective-permute-start | bytes 368648 | tf_op jit(solution)/shard_map/ppermute | solution.py:599
  131.3 7.7 %collective-permute-start.27 = (bf16[144,768]{1,0:T(8,128)(2,1)S(1)}, bf16[144,768]{1,0:T(8,128)(2,1)S(1)}, u32[]{:S(2)}, u32[]{:S(2)}) collective-permute-start(bf16[144,768]{1,0:T(8,128)(2,1)S(1)} %shard_map.361.own), channel_id=1, source_target_pairs={{0,16},{1,9},{2,18},{3,11},{4,20},{5,13},{6,22},{7,15},{8,24},{9,1... | collective-permute-start | bytes 663560 | tf_op jit(solution)/shard_map/ppermute | solution.py:590
  134.0 4.9 %collective-permute-start.28 = (bf16[80,768]{1,0:T(8,128)(2,1)S(1)}, bf16[80,768]{1,0:T(8,128)(2,1)S(1)}, u32[]{:S(2)}, u32[]{:S(2)}) collective-permute-start(bf16[80,768]{1,0:T(8,128)(2,1)S(1)} %shard_map.364.own), channel_id=1, source_target_pairs={{0,16},{1,9},{2,18},{3,11},{4,20},{5,13},{6,22},{7,15},{8,24},{9,1... | collective-permute-start | bytes 368648 | tf_op jit(solution)/shard_map/ppermute | solution.py:590
  139.1 13.3 %collective-permute-start.31 = (bf16[2,144,768]{2,1,0:T(8,128)(2,1)S(1)}, bf16[2,144,768]{2,1,0:T(8,128)(2,1)S(1)}, u32[]{:S(2)}, u32[]{:S(2)}) collective-permute-start(bf16[2,144,768]{2,1,0:T(8,128)(2,1)S(1)} %shard_map.367.own), channel_id=1, source_target_pairs={{0,8},{1,17},{2,10},{3,19},{4,12},{5,21},{6,14},{7,23},{8,0},{9,25... | collective-permute-start | bytes 1327112 | tf_op jit(solution)/shard_map/ppermute | solution.py:590
  140.6 6.3 %collective-permute-start.30 = (bf16[80,768]{1,0:T(8,128)(2,1)S(1)}, bf16[80,768]{1,0:T(8,128)(2,1)S(1)}, u32[]{:S(2)}, u32[]{:S(2)}) collective-permute-start(bf16[80,768]{1,0:T(8,128)(2,1)S(1)} %shard_map.362.own), channel_id=1, source_target_pairs={{0,16},{1,9},{2,18},{3,11},{4,20},{5,13},{6,22},{7,15},{8,24},{9,1... | collective-permute-start | bytes 368648 | tf_op jit(solution)/shard_map/ppermute | solution.py:590
  141.6 8.5 %collective-permute-start.29 = (bf16[2,80,768]{2,1,0:T(8,128)(2,1)S(1)}, bf16[2,80,768]{2,1,0:T(8,128)(2,1)S(1)}, u32[]{:S(2)}, u32[]{:S(2)}) collective-permute-start(bf16[2,80,768]{2,1,0:T(8,128)(2,1)S(1)} %shard_map.365.own), channel_id=1, source_target_pairs={{0,8},{1,17},{2,10},{3,19},{4,12},{5,21},{6,14},{7,23},{8,0},{9,25... | collective-permute-start | bytes 737288 | tf_op jit(solution)/shard_map/ppermute | solution.py:590
  146.9 6.3 %collective-permute-start.32 = (bf16[2,80,768]{2,1,0:T(8,128)(2,1)S(1)}, bf16[2,80,768]{2,1,0:T(8,128)(2,1)S(1)}, u32[]{:S(2)}, u32[]{:S(2)}) collective-permute-start(bf16[2,80,768]{2,1,0:T(8,128)(2,1)S(1)} %shard_map.368.own), channel_id=1, source_target_pairs={{0,8},{1,17},{2,10},{3,19},{4,12},{5,21},{6,14},{7,23},{8,0},{9,25... | collective-permute-start | bytes 737288 | tf_op jit(solution)/shard_map/ppermute | solution.py:590
  (24 other events, 225.3 us)
where the time goes:
time: 156 us; the launch traced here: 155 us
  Pallas kernels  62.5 us (40%)
  waiting for transfers between devices  46 us (29%)
  starting transfers between devices  40.9 us (26%)
  local copies, waits for them, and re-layouts  4.92 us (3%)
    pallas_call x30, Pallas kernels, call(): pl.pallas_call(kernel, out_shape=[jax.ShapeDtypeStruct(s, d) for s, d in...  62.5 us
    ppermute x12, waiting for transfers between devices, swap_first(): return lax.ppermute(array, ('blk', 'batch'), perm)  31.7 us
    ppermute x6, starting transfers between devices, swap_z(): lax.ppermute(array, 'batch', [(i, i ^ (2 if (i % 2 == 0) == first else 4)...  14.6 us
    ppermute x12, starting transfers between devices, swap_first(): return lax.ppermute(array, ('blk', 'batch'), perm)  12.7 us
    ppermute x9, starting transfers between devices, swap(): lax.ppermute(array, 'blk', [(i, i ^ bit) for i in range(lax.axis_size('bl...  11.7 us
    ppermute x6, waiting for transfers between devices, swap_z(): lax.ppermute(array, 'batch', [(i, i ^ (2 if (i % 2 == 0) == first else 4)...  9.12 us
    ppermute x6, waiting for transfers between devices, swap_batch(): lax.ppermute(array, 'batch', [(i, i ^ bit) for i in range(lax.axis_size('...  5.08 us
  transfers between devices with their start and end apart: 33, of which 16 were waited for; matrix products, arithmetic and copies ran while one was open for 1% of the time, Pallas kernels for 26%

commit v1 on v0

--- a/solution.py
+++ b/solution.py
@@ -159,8 +159,8 @@
 
 
 def gelu_both(v):
-    e = jnp.exp(v * v * -0.5)
-    t = 1.0 / (1.0 + (0.3275911 * 0.7071067811865476) * jnp.abs(v))
+    e = jnp.exp2(v * v * -0.7213475204444817)
+    t = pl.reciprocal(1.0 + (0.3275911 * 0.7071067811865476) * jnp.abs(v))
     poly = t * (0.5 * 0.254829592 + t * (0.5 * -0.284496736 + t * (0.5 * 1.421413741 + t * (0.5 * -1.453152027 + t * (0.5 * 1.061405429)))))
     tail = poly * e
     phi = jnp.where(v >= 0, 1.0 - tail, tail)

time: 156 us -> 156 us (level)
  no operation moved by 1% of the time
where the time goes in v1:
time: 156 us; the launch traced here: 155 us
  Pallas kernels  62.3 us (40%)
  waiting for transfers between devices  46 us (29%)
  starting transfers between devices  40.8 us (26%)
  local copies, waits for them, and re-layouts  4.92 us (3%)
    pallas_call x30, Pallas kernels, call(): pl.pallas_call(kernel, out_shape=[jax.ShapeDtypeStruct(s, d) for s, d in...  62.3 us
    ppermute x12, waiting for transfers between devices, swap_first(): return lax.ppermute(array, ('blk', 'batch'), perm)  31.7 us
    ppermute x6, starting transfers between devices, swap_z(): lax.ppermute(array, 'batch', [(i, i ^ (2 if (i % 2 == 0) == first else 4)...  14.6 us
    ppermute x12, starting transfers between devices, swap_first(): return lax.ppermute(array, ('blk', 'batch'), perm)  12.7 us
    ppermute x9, starting transfers between devices, swap(): lax.ppermute(array, 'blk', [(i, i ^ bit) for i in range(lax.axis_size('bl...  11.7 us
    ppermute x6, waiting for transfers between devices, swap_z(): lax.ppermute(array, 'batch', [(i, i ^ (2 if (i % 2 == 0) == first else 4)...  9.16 us
    ppermute x6, waiting for transfers between devices, swap_batch(): lax.ppermute(array, 'batch', [(i, i ^ bit) for i in range(lax.axis_size('...  5.08 us
  transfers between devices with their start and end apart: 33, of which 16 were waited for; matrix products, arithmetic and copies ran while one was open for 1% of the time, Pallas kernels for 26%

profile of v1, /device:TPU:0, one launch (start us, length us, event | category | flops | bytes accessed | tf_op | source)
XLA Modules:
  0.0 155.3 jit_solution(5881712029691491467)
XLA Ops:
  2.0 3.0 %collective-permute-start = (bf16[128,768]{1,0:T(8,128)(2,1)S(1)}, bf16[128,768]{1,0:T(8,128)(2,1)S(1)}, u32[]{:S(2)}, u32[]{:S(2)}) collective-permute-start(bf16[128,768]{1,0:T(8,128)(2,1)S(1)} %get-tuple-element.332), channel_id=1, source_target_pairs={{0,8},{8,0},{16,24},{24,16},{1,9},{9,1},{17,25},{25,17},{2,10},{10... | collective-permute-start | bytes 589832 | tf_op jit(solution)/shard_map/ppermute | solution.py:580
  5.0 1.5 collective-permute-start.1
  8.9 3.8 %shard_map.341 = (bf16[512,768]{1,0:T(8,128)(2,1)S(1)}, f32[512,128]{1,0:T(8,128)S(1)}) custom-call(s32[4,80]{1,0:T(4,128)S(1)} %copy-done.9, s32[4]{0:T(128)S(1)} %copy-done.18, s32[4,80]{1,0:T(4,128)S(1)} %copy-done.10, bf16[15360,768]{1,0:T(8,128)(2,1)} %table_ref.1), custom_call_target="tpu_custom_call" | custom-call | flops 1024 | bytes 1024 | tf_op jit(solution)/shard_map/pallas_call | solution.py:503
  12.7 1.9 %collective-permute-start.3 = (bf16[128,768]{1,0:T(8,128)(2,1)S(1)}, bf16[128,768]{1,0:T(8,128)(2,1)S(1)}, u32[]{:S(2)}, u32[]{:S(2)}) collective-permute-start(bf16[128,768]{1,0:T(8,128)(2,1)S(1)} %get-tuple-element.329), channel_id=1, source_target_pairs={{0,8},{8,0},{16,24},{24,16},{1,9},{9,1},{17,25},{25,17},{2,10},{10... | collective-permute-start | bytes 589832 | tf_op jit(solution)/shard_map/ppermute | solution.py:580
  14.6 1.5 collective-permute-start.4
  16.4 9.4 %shard_map.342 = (bf16[768,512]{1,0:T(8,128)(2,1)S(1)}, bf16[512,768]{1,0:T(8,128)(2,1)S(1)}, bf16[512,768]{1,0:T(8,128)(2,1)S(1)}, bf16[512,768]{1,0:T(8,128)(2...) custom-call(s32[4]{0:T(128)S(1)} %copy-done.8, ...), custom_call_target="tpu_custom_call" | custom-call | flops 1024 | bytes 1024 | tf_op jit(solution)/shard_map/pallas_call | solution.py:503
  26.0 19.3 %shard_map.343 = (bf16[512,768]{1,0:T(8,128)(2,1)S(1)}, bf16[4,4,80,768]{3,2,1,0:T(8,128)(2,1)S(1)}, bf16[4,4,80,768]{3,2,1,0:T(8,128)(2,1)S(1)}, bf16[4,4,112,7...) custom-call(f32[512,768]{1,0:T(8,128)S(1)} %get-tuple-element.175.n_, ...), custom_call_target="tpu_custom_call" | custom-call | flops 1024 | bytes 1024 | tf_op jit(solution)/shard_map/pallas_call | solution.py:503
  45.9 5.0 %shard_map.344 = (bf16[4,4,32,768]{3,2,1,0:T(8,128)(2,1)S(1)}, bf16[4,4,32,768]{3,2,1,0:T(8,128)(2,1)S(1)}, f32[512,768]{1,0:T(8,128)S(1)}, bf16[512,768]{1,0:T(8,128)(2,1)S(1)}, f32[16,768]{1,0:T(8,128)S(1)}) custom-call(f32[512,768]{1,0:T(8,128)S(1)} %get-tuple-element.175.n_ref, f32[512,128]{1,0:T(8,128)S(1)} %get-tuple-element.180.rstd_ref, ...), custom_call_target="tpu_custom_call" | custom-call | flops 1024 | bytes 1024 | tf_op jit(solution)/shard_map/pallas_call | solution.py:503
  55.3 1.9 %collective-permute-start.9 = (bf16[8,144,768]{2,1,0:T(8,128)(2,1)S(1)}, bf16[8,144,768]{2,1,0:T(8,128)(2,1)S(1)}, u32[]{:S(2)}, u32[]{:S(2)}) collective-permute-start(bf16[8,144,768]{2,1,0:T(8,128)(2,1)S(1)} %get-tuple-element.204), channel_id=1, source_target_pairs={{0,8},{1,17},{2,10},{3,19},{4,12},{5,21},{6,14},{7,23},{8,0},{9,25... | collective-permute-start | bytes 5308424 | tf_op jit(solution)/shard_map/ppermute | solution.py:590
  57.2 1.6 %collective-permute-start.10 = (bf16[8,80,768]{2,1,0:T(8,128)(2,1)S(1)}, bf16[8,80,768]{2,1,0:T(8,128)(2,1)S(1)}, u32[]{:S(2)}, u32[]{:S(2)}) collective-permute-start(bf16[8,80,768]{2,1,0:T(8,128)(2,1)S(1)} %get-tuple-element.206), channel_id=1, source_target_pairs={{0,2},{1,5},{2,0},{3,7},{4,6},{5,1},{6,4},{7,3},{8,10},{9,13},{10,... | collective-permute-start | bytes 2949128 | tf_op jit(solution)/shard_map/ppermute | solution.py:599
  58.7 8.8 %shard_map.348 = (bf16[512,512]{1,0:T(8,128)(2,1)S(1)}, bf16[512,512]{1,0:T(8,128)(2,1)S(1)}, bf16[512,512]{1,0:T(8,128)(2,1)S(1)}, bf16[4,4,80,512]{3,2,1,0:T(8...) custom-call(s32[4]{0:T(128)S(1)} %copy-done.8, ...), custom_call_target="tpu_custom_call" | custom-call | flops 1024 | bytes 1024 | tf_op jit(solution)/shard_map/pallas_call | solution.py:503
  67.5 4.8 %shard_map.349 = (bf16[512,256]{1,0:T(8,128)(2,1)S(1)}, bf16[512,256]{1,0:T(8,128)(2,1)S(1)}, bf16[512,256]{1,0:T(8,128)(2,1)S(1)}, bf16[4,4,80,256]{3,2,1,0:T(8,128)(2,1)S(1)}, bf16[4,4,80,256]{3,2,1,0:T(8,128)(2,1)S(1)}) custom-call(s32[4]{0:T(128)S(1)} %copy-done.8, bf16[768,512]{1,0:T(8,128)(2,1)S(1)} %get-tuple-element.207.x_t_ref, ...), custom_call_target="tpu_custom_call" | custom-call | flops 1024 | bytes 1024 | tf_op jit(solution)/shard_map/pallas_call | solution.py:503
  77.1 1.5 collective-permute-start.15
  78.6 2.9 %collective-permute-done.10 = bf16[8,80,768]{2,1,0:T(8,128)(2,1)S(1)} collective-permute-done((bf16[8,80,768]{2,1,0:T(8,128)(2,1)S(1)}, bf16[8,80,768]{2,1,0:T(8,128)(2,1)S(1)}, u32[]{:S(2)}, u32[]{:S(2)}) %collective-permute-start.10) | collective-permute-done | bytes 983072 | tf_op jit(solution)/shard_map/ppermute | solution.py:599
  82.3 3.3 %collective-permute-start.17 = (bf16[4,80,768]{2,1,0:T(8,128)(2,1)S(1)}, bf16[4,80,768]{2,1,0:T(8,128)(2,1)S(1)}, u32[]{:S(2)}, u32[]{:S(2)}) collective-permute-start(bf16[4,80,768]{2,1,0:T(8,128)(2,1)S(1)} %get-tuple-element.254), channel_id=1, source_target_pairs={{0,4},{1,3},{2,6},{3,1},{4,0},{5,7},{6,2},{7,5},{8,12},{9,11},{10,... | collective-permute-start | bytes 1474568 | tf_op jit(solution)/shard_map/ppermute | solution.py:599
  85.6 2.1 %shard_map.353 = (bf16[512,768]{1,0:T(8,128)(2,1)S(1)}, bf16[2,128,768]{2,1,0:T(8,128)(2,1)S(1)}, bf16[2,128,768]{2,1,0:T(8,128)(2,1)S(1)}, bf16[2,128,768]{2,1,0:T(8,128)(2,1)S(1)}) custom-call(f32[512,128]{1,0:T(8,128)S(1)} %get-tuple-element.238.hit_ref, bf16[512,768]{1,0:T(8,128)(2,1)S(1)} %get-tuple-element.239.out_page, ...), custom_call_target="tpu_custom_call" | custom-call | flops 1024 | bytes 1024 | tf_op jit(solution)/shard_map/pallas_call | solution.py:503
  87.8 9.9 %collective-permute-done.15 = bf16[8,80,768]{2,1,0:T(8,128)(2,1)S(1)} collective-permute-done((bf16[8,80,768]{2,1,0:T(8,128)(2,1)S(1)}, bf16[8,80,768]{2,1,0:T(8,128)(2,1)S(1)}, u32[]{:S(2)}, u32[]{:S(2)}) %collective-permute-start.15) | collective-permute-done | bytes 983072 | tf_op jit(solution)/shard_map/ppermute | solution.py:590
  97.9 1.9 %collective-permute-start.16 = (bf16[4,80,768]{2,1,0:T(8,128)(2,1)S(1)}, bf16[4,80,768]{2,1,0:T(8,128)(2,1)S(1)}, u32[]{:S(2)}, u32[]{:S(2)}) collective-permute-start(bf16[4,80,768]{2,1,0:T(8,128)(2,1)S(1)} %get-tuple-element.252), channel_id=1, source_target_pairs={{0,16},{1,9},{2,18},{3,11},{4,20},{5,13},{6,22},{7,15},{8,24},{9,1... | collective-permute-start | bytes 1474568 | tf_op jit(solution)/shard_map/ppermute | solution.py:590
  100.4 1.6 %collective-permute-start.19 = (bf16[2,144,768]{2,1,0:T(8,128)(2,1)S(1)}, bf16[2,144,768]{2,1,0:T(8,128)(2,1)S(1)}, u32[]{:S(2)}, u32[]{:S(2)}) collective-permute-start(bf16[2,144,768]{2,1,0:T(8,128)(2,1)S(1)} %get-tuple-element.264), channel_id=1, source_target_pairs={{0,2},{1,5},{2,0},{3,7},{4,6},{5,1},{6,4},{7,3},{8,10},{9,13},{10,... | collective-permute-start | bytes 1327112 | tf_op jit(solution)/shard_map/ppermute | solution.py:599
  102.1 1.5 collective-permute-start.18
  103.7 4.1 %collective-permute-done.16 = bf16[4,80,768]{2,1,0:T(8,128)(2,1)S(1)} collective-permute-done((bf16[4,80,768]{2,1,0:T(8,128)(2,1)S(1)}, bf16[4,80,768]{2,1,0:T(8,128)(2,1)S(1)}, u32[]{:S(2)}, u32[]{:S(2)}) %collective-permute-start.16) | collective-permute-done | bytes 491552 | tf_op jit(solution)/shard_map/ppermute | solution.py:590
  108.0 3.7 %collective-permute-start.21 = (bf16[2,80,768]{2,1,0:T(8,128)(2,1)S(1)}, bf16[2,80,768]{2,1,0:T(8,128)(2,1)S(1)}, u32[]{:S(2)}, u32[]{:S(2)}) collective-permute-start(bf16[2,80,768]{2,1,0:T(8,128)(2,1)S(1)} %get-tuple-element.274), channel_id=1, source_target_pairs={{0,2},{1,5},{2,0},{3,7},{4,6},{5,1},{6,4},{7,3},{8,10},{9,13},{10,... | collective-permute-start | bytes 737288 | tf_op jit(solution)/shard_map/ppermute | solution.py:599
  113.6 1.6 %collective-permute-start.25 = (bf16[2,128,768]{2,1,0:T(8,128)(2,1)S(1)}, bf16[2,128,768]{2,1,0:T(8,128)(2,1)S(1)}, u32[]{:S(2)}, u32[]{:S(2)}) collective-permute-start(bf16[2,128,768]{2,1,0:T(8,128)(2,1)S(1)} %get-tuple-element.286), channel_id=1, source_target_pairs={{0,24},{8,16},{16,8},{24,0},{1,25},{9,17},{17,9},{25,1},{2,26},{10... | collective-permute-start | bytes 1179656 | tf_op jit(solution)/shard_map/ppermute | solution.py:580
  115.3 1.9 %collective-permute-start.20 = (bf16[1,144,768]{2,1,0:T(8,128)(2,1)S(1)}, bf16[1,144,768]{2,1,0:T(8,128)(2,1)S(1)}, u32[]{:S(2)}, u32[]{:S(2)}) collective-permute-start(bf16[1,144,768]{2,1,0:T(8,128)(2,1)S(1)} %get-tuple-element.272), channel_id=1, source_target_pairs={{0,4},{1,3},{2,6},{3,1},{4,0},{5,7},{6,2},{7,5},{8,12},{9,11},{10,... | collective-permute-start | bytes 663560 | tf_op jit(solution)/shard_map/ppermute | solution.py:599
  117.3 2.1 %collective-permute-done.21 = bf16[2,80,768]{2,1,0:T(8,128)(2,1)S(1)} collective-permute-done((bf16[2,80,768]{2,1,0:T(8,128)(2,1)S(1)}, bf16[2,80,768]{2,1,0:T(8,128)(2,1)S(1)}, u32[]{:S(2)}, u32[]{:S(2)}) %collective-permute-start.21) | collective-permute-done | bytes 245792 | tf_op jit(solution)/shard_map/ppermute | solution.py:599
  119.5 4.2 %collective-permute-done.20.came = bf16[1,144,768]{2,1,0:T(8,128)(2,1)S(1)} collective-permute-done((bf16[1,144,768]{2,1,0:T(8,128)(2,1)S(1)}, bf16[1,144,768]{2,1,0:T(8,128)(2,1)S(1)}, u32[]{:S(2)}, u32[]{:S(2)}) %collective-permute-start.20) | collective-permute-done | bytes 221216 | tf_op jit(solution)/shard_map/ppermute | solution.py:599
  123.7 2.4 %collective-permute-start.22 = (bf16[1,80,768]{2,1,0:T(8,128)(2,1)S(1)}, bf16[1,80,768]{2,1,0:T(8,128)(2,1)S(1)}, u32[]{:S(2)}, u32[]{:S(2)}) collective-permute-start(bf16[1,80,768]{2,1,0:T(8,128)(2,1)S(1)} %get-tuple-element.282), channel_id=1, source_target_pairs={{0,4},{1,3},{2,6},{3,1},{4,0},{5,7},{6,2},{7,5},{8,12},{9,11},{10,... | collective-permute-start | bytes 368648 | tf_op jit(solution)/shard_map/ppermute | solution.py:599
  126.1 5.0 %collective-permute-done.26.came = bf16[1,80,768]{2,1,0:T(8,128)(2,1)S(1)} collective-permute-done((bf16[1,80,768]{2,1,0:T(8,128)(2,1)S(1)}, bf16[1,80,768]{2,1,0:T(8,128)(2,1)S(1)}, u32[]{:S(2)}, u32[]{:S(2)}) %collective-permute-start.26) | collective-permute-done | bytes 122912 | tf_op jit(solution)/shard_map/ppermute | solution.py:590
  134.6 4.2 %collective-permute-done.28.came = bf16[80,768]{1,0:T(8,128)(2,1)S(1)} collective-permute-done((bf16[80,768]{1,0:T(8,128)(2,1)S(1)}, bf16[80,768]{1,0:T(8,128)(2,1)S(1)}, u32[]{:S(2)}, u32[]{:S(2)}) %collective-permute-start.28) | collective-permute-done | bytes 122912 | tf_op jit(solution)/shard_map/ppermute | solution.py:590
  138.9 1.6 %collective-permute-start.31 = (bf16[2,144,768]{2,1,0:T(8,128)(2,1)S(1)}, bf16[2,144,768]{2,1,0:T(8,128)(2,1)S(1)}, u32[]{:S(2)}, u32[]{:S(2)}) collective-permute-start(bf16[2,144,768]{2,1,0:T(8,128)(2,1)S(1)} %shard_map.367.own), channel_id=1, source_target_pairs={{0,8},{1,17},{2,10},{3,19},{4,12},{5,21},{6,14},{7,23},{8,0},{9,25... | collective-permute-start | bytes 1327112 | tf_op jit(solution)/shard_map/ppermute | solution.py:590
  141.9 4.8 %collective-permute-done.30.came = bf16[80,768]{1,0:T(8,128)(2,1)S(1)} collective-permute-done((bf16[80,768]{1,0:T(8,128)(2,1)S(1)}, bf16[80,768]{1,0:T(8,128)(2,1)S(1)}, u32[]{:S(2)}, u32[]{:S(2)}) %collective-permute-start.30) | collective-permute-done | bytes 122912 | tf_op jit(solution)/shard_map/ppermute | solution.py:590
  147.3 2.6 %collective-permute-done.29.came = bf16[2,80,768]{2,1,0:T(8,128)(2,1)S(1)} collective-permute-done((bf16[2,80,768]{2,1,0:T(8,128)(2,1)S(1)}, bf16[2,80,768]{2,1,0:T(8,128)(2,1)S(1)}, u32[]{:S(2)}, u32[]{:S(2)}) %collective-permute-start.29) | collective-permute-done | bytes 245792 | tf_op jit(solution)/shard_map/ppermute | solution.py:590
  (118 shorter events, 28.7 us)
Async XLA Ops:
  2.0 14.1 %collective-permute-start = (bf16[128,768]{1,0:T(8,128)(2,1)S(1)}, bf16[128,768]{1,0:T(8,128)(2,1)S(1)}, u32[]{:S(2)}, u32[]{:S(2)}) collective-permute-start(bf16[128,768]{1,0:T(8,128)(2,1)S(1)} %get-tuple-element.332), channel_id=1, source_target_pairs={{0,8},{8,0},{16,24},{24,16},{1,9},{9,1},{17,25},{25,17},{2,10},{10... | collective-permute-start | bytes 589832 | tf_op jit(solution)/shard_map/ppermute | solution.py:580
  5.0 11.2 %collective-permute-start.1 = (bf16[128,768]{1,0:T(8,128)(2,1)S(1)}, bf16[128,768]{1,0:T(8,128)(2,1)S(1)}, u32[]{:S(2)}, u32[]{:S(2)}) collective-permute-start(bf16[128,768]{1,0:T(8,128)(2,1)S(1)} %get-tuple-element.331), channel_id=1, source_target_pairs={{0,16},{8,24},{16,0},{24,8},{1,17},{9,25},{17,1},{25,9},{2,18},{10... | collective-permute-start | bytes 589832 | tf_op jit(solution)/shard_map/ppermute | solution.py:580
  6.6 9.7 %collective-permute-start.2 = (bf16[128,768]{1,0:T(8,128)(2,1)S(1)}, bf16[128,768]{1,0:T(8,128)(2,1)S(1)}, u32[]{:S(2)}, u32[]{:S(2)}) collective-permute-start(bf16[128,768]{1,0:T(8,128)(2,1)S(1)} %get-tuple-element.330), channel_id=1, source_target_pairs={{0,24},{8,16},{16,8},{24,0},{1,25},{9,17},{17,9},{25,1},{2,26},{10... | collective-permute-start | bytes 589832 | tf_op jit(solution)/shard_map/ppermute | solution.py:580
  12.7 13.2 %collective-permute-start.3 = (bf16[128,768]{1,0:T(8,128)(2,1)S(1)}, bf16[128,768]{1,0:T(8,128)(2,1)S(1)}, u32[]{:S(2)}, u32[]{:S(2)}) collective-permute-start(bf16[128,768]{1,0:T(8,128)(2,1)S(1)} %get-tuple-element.329), channel_id=1, source_target_pairs={{0,8},{8,0},{16,24},{24,16},{1,9},{9,1},{17,25},{25,17},{2,10},{10... | collective-permute-start | bytes 589832 | tf_op jit(solution)/shard_map/ppermute | solution.py:580
  14.6 11.3 %collective-permute-start.4 = (bf16[128,768]{1,0:T(8,128)(2,1)S(1)}, bf16[128,768]{1,0:T(8,128)(2,1)S(1)}, u32[]{:S(2)}, u32[]{:S(2)}) collective-permute-start(bf16[128,768]{1,0:T(8,128)(2,1)S(1)} %get-tuple-element.328), channel_id=1, source_target_pairs={{0,16},{8,24},{16,0},{24,8},{1,17},{9,25},{17,1},{25,9},{2,18},{10... | collective-permute-start | bytes 589832 | tf_op jit(solution)/shard_map/ppermute | solution.py:580
  16.1 9.8 %collective-permute-start.5 = (bf16[128,768]{1,0:T(8,128)(2,1)S(1)}, bf16[128,768]{1,0:T(8,128)(2,1)S(1)}, u32[]{:S(2)}, u32[]{:S(2)}) collective-permute-start(bf16[128,768]{1,0:T(8,128)(2,1)S(1)} %get-tuple-element.327), channel_id=1, source_target_pairs={{0,24},{8,16},{16,8},{24,0},{1,25},{9,17},{17,9},{25,1},{2,26},{10... | collective-permute-start | bytes 589832 | tf_op jit(solution)/shard_map/ppermute | solution.py:580
  45.3 9.1 %collective-permute-start.7 = (bf16[4,4,112,768]{3,2,1,0:T(8,128)(2,1)S(1)}, bf16[4,4,112,768]{3,2,1,0:T(8,128)(2,1)S(1)}, u32[]{:S(2)}, u32[]{:S(2)}) collective-permute-start(bf16[4,4,112,768]{3,2,1,0:T(8,128)(2,1)S(1)} %get-tuple-element.193), channel_id=1, source_target_pairs={{0,1},{1,0},{2,3},{3,2},{4,5},{5,4},{6,7},{7,6},{8,9},{9,8},{10,11... | collective-permute-start | bytes 8257544 | tf_op jit(solution)/shard_map/ppermute | solution.py:594
  45.4 7.9 %collective-permute-start.6 = (bf16[4,4,80,768]{3,2,1,0:T(8,128)(2,1)S(1)}, bf16[4,4,80,768]{3,2,1,0:T(8,128)(2,1)S(1)}, u32[]{:S(2)}, u32[]{:S(2)}) collective-permute-start(bf16[4,4,80,768]{3,2,1,0:T(8,128)(2,1)S(1)} %get-tuple-element.178), channel_id=1, source_target_pairs={{0,1},{1,0},{2,3},{3,2},{4,5},{5,4},{6,7},{7,6},{8,9},{9,8},{10,11... | collective-permute-start | bytes 5898248 | tf_op jit(solution)/shard_map/ppermute | solution.py:594
  50.9 3.5 %collective-permute-start.8 = (bf16[4,4,32,768]{3,2,1,0:T(8,128)(2,1)S(1)}, bf16[4,4,32,768]{3,2,1,0:T(8,128)(2,1)S(1)}, u32[]{:S(2)}, u32[]{:S(2)}) collective-permute-start(bf16[4,4,32,768]{3,2,1,0:T(8,128)(2,1)S(1)} %get-tuple-element.194), channel_id=1, source_target_pairs={{0,1},{1,0},{2,3},{3,2},{4,5},{5,4},{6,7},{7,6},{8,9},{9,8},{10,11... | collective-permute-start | bytes 2359304 | tf_op jit(solution)/shard_map/ppermute | solution.py:594
  55.3 26.5 %collective-permute-start.9 = (bf16[8,144,768]{2,1,0:T(8,128)(2,1)S(1)}, bf16[8,144,768]{2,1,0:T(8,128)(2,1)S(1)}, u32[]{:S(2)}, u32[]{:S(2)}) collective-permute-start(bf16[8,144,768]{2,1,0:T(8,128)(2,1)S(1)} %get-tuple-element.204), channel_id=1, source_target_pairs={{0,8},{1,17},{2,10},{3,19},{4,12},{5,21},{6,14},{7,23},{8,0},{9,25... | collective-permute-start | bytes 5308424 | tf_op jit(solution)/shard_map/ppermute | solution.py:590
  57.2 24.3 %collective-permute-start.10 = (bf16[8,80,768]{2,1,0:T(8,128)(2,1)S(1)}, bf16[8,80,768]{2,1,0:T(8,128)(2,1)S(1)}, u32[]{:S(2)}, u32[]{:S(2)}) collective-permute-start(bf16[8,80,768]{2,1,0:T(8,128)(2,1)S(1)} %get-tuple-element.206), channel_id=1, source_target_pairs={{0,2},{1,5},{2,0},{3,7},{4,6},{5,1},{6,4},{7,3},{8,10},{9,13},{10,... | collective-permute-start | bytes 2949128 | tf_op jit(solution)/shard_map/ppermute | solution.py:599
  73.0 2.7 %collective-permute-start.11 = (bf16[2,4,80,512]{3,2,1,0:T(8,128)(2,1)S(1)}, bf16[2,4,80,512]{3,2,1,0:T(8,128)(2,1)S(1)}, u32[]{:S(2)}, u32[]{:S(2)}) collective-permute-start(bf16[2,4,80,512]{3,2,1,0:T(8,128)(2,1)S(1)} %get-tuple-element.219), channel_id=1, source_target_pairs={{0,1},{1,0},{2,3},{3,2},{4,5},{5,4},{6,7},{7,6},{8,9},{9,8},{10,11... | collective-permute-start | bytes 1966088 | tf_op jit(solution)/shard_map/ppermute | solution.py:594
  73.1 3.5 %collective-permute-start.12 = (bf16[2,4,80,512]{3,2,1,0:T(8,128)(2,1)S(1)}, bf16[2,4,80,512]{3,2,1,0:T(8,128)(2,1)S(1)}, u32[]{:S(2)}, u32[]{:S(2)}) collective-permute-start(bf16[2,4,80,512]{3,2,1,0:T(8,128)(2,1)S(1)} %get-tuple-element.220), channel_id=1, source_target_pairs={{0,1},{1,0},{2,3},{3,2},{4,5},{5,4},{6,7},{7,6},{8,9},{9,8},{10,11... | collective-permute-start | bytes 1966088 | tf_op jit(solution)/shard_map/ppermute | solution.py:594
  77.1 20.6 %collective-permute-start.15 = (bf16[8,80,768]{2,1,0:T(8,128)(2,1)S(1)}, bf16[8,80,768]{2,1,0:T(8,128)(2,1)S(1)}, u32[]{:S(2)}, u32[]{:S(2)}) collective-permute-start(bf16[8,80,768]{2,1,0:T(8,128)(2,1)S(1)} %get-tuple-element.237), channel_id=1, source_target_pairs={{0,8},{1,17},{2,10},{3,19},{4,12},{5,21},{6,14},{7,23},{8,0},{9,25... | collective-permute-start | bytes 2949128 | tf_op jit(solution)/shard_map/ppermute | solution.py:590
  82.2 17.9 %collective-permute-start.14 = (bf16[4,144,768]{2,1,0:T(8,128)(2,1)S(1)}, bf16[4,144,768]{2,1,0:T(8,128)(2,1)S(1)}, u32[]{:S(2)}, u32[]{:S(2)}) collective-permute-start(bf16[4,144,768]{2,1,0:T(8,128)(2,1)S(1)} %get-tuple-element.235), channel_id=1, source_target_pairs={{0,16},{1,9},{2,18},{3,11},{4,20},{5,13},{6,22},{7,15},{8,24},{9,1... | collective-permute-start | bytes 2654216 | tf_op jit(solution)/shard_map/ppermute | solution.py:590
  82.3 19.7 %collective-permute-start.17 = (bf16[4,80,768]{2,1,0:T(8,128)(2,1)S(1)}, bf16[4,80,768]{2,1,0:T(8,128)(2,1)S(1)}, u32[]{:S(2)}, u32[]{:S(2)}) collective-permute-start(bf16[4,80,768]{2,1,0:T(8,128)(2,1)S(1)} %get-tuple-element.254), channel_id=1, source_target_pairs={{0,4},{1,3},{2,6},{3,1},{4,0},{5,7},{6,2},{7,5},{8,12},{9,11},{10,... | collective-permute-start | bytes 1474568 | tf_op jit(solution)/shard_map/ppermute | solution.py:599
  97.9 9.9 %collective-permute-start.16 = (bf16[4,80,768]{2,1,0:T(8,128)(2,1)S(1)}, bf16[4,80,768]{2,1,0:T(8,128)(2,1)S(1)}, u32[]{:S(2)}, u32[]{:S(2)}) collective-permute-start(bf16[4,80,768]{2,1,0:T(8,128)(2,1)S(1)} %get-tuple-element.252), channel_id=1, source_target_pairs={{0,16},{1,9},{2,18},{3,11},{4,20},{5,13},{6,22},{7,15},{8,24},{9,1... | collective-permute-start | bytes 1474568 | tf_op jit(solution)/shard_map/ppermute | solution.py:590
  100.4 13.2 %collective-permute-start.19 = (bf16[2,144,768]{2,1,0:T(8,128)(2,1)S(1)}, bf16[2,144,768]{2,1,0:T(8,128)(2,1)S(1)}, u32[]{:S(2)}, u32[]{:S(2)}) collective-permute-start(bf16[2,144,768]{2,1,0:T(8,128)(2,1)S(1)} %get-tuple-element.264), channel_id=1, source_target_pairs={{0,2},{1,5},{2,0},{3,7},{4,6},{5,1},{6,4},{7,3},{8,10},{9,13},{10,... | collective-permute-start | bytes 1327112 | tf_op jit(solution)/shard_map/ppermute | solution.py:599
  102.1 13.2 %collective-permute-start.18 = (bf16[2,80,768]{2,1,0:T(8,128)(2,1)S(1)}, bf16[2,80,768]{2,1,0:T(8,128)(2,1)S(1)}, u32[]{:S(2)}, u32[]{:S(2)}) collective-permute-start(bf16[2,80,768]{2,1,0:T(8,128)(2,1)S(1)} %get-tuple-element.262), channel_id=1, source_target_pairs={{0,8},{1,17},{2,10},{3,19},{4,12},{5,21},{6,14},{7,23},{8,0},{9,25... | collective-permute-start | bytes 737288 | tf_op jit(solution)/shard_map/ppermute | solution.py:590
  108.0 11.5 %collective-permute-start.21 = (bf16[2,80,768]{2,1,0:T(8,128)(2,1)S(1)}, bf16[2,80,768]{2,1,0:T(8,128)(2,1)S(1)}, u32[]{:S(2)}, u32[]{:S(2)}) collective-permute-start(bf16[2,80,768]{2,1,0:T(8,128)(2,1)S(1)} %get-tuple-element.274), channel_id=1, source_target_pairs={{0,2},{1,5},{2,0},{3,7},{4,6},{5,1},{6,4},{7,3},{8,10},{9,13},{10,... | collective-permute-start | bytes 737288 | tf_op jit(solution)/shard_map/ppermute | solution.py:599
  111.7 20.8 %collective-permute-start.23 = (bf16[2,128,768]{2,1,0:T(8,128)(2,1)S(1)}, bf16[2,128,768]{2,1,0:T(8,128)(2,1)S(1)}, u32[]{:S(2)}, u32[]{:S(2)}) collective-permute-start(bf16[2,128,768]{2,1,0:T(8,128)(2,1)S(1)} %get-tuple-element.284), channel_id=1, source_target_pairs={{0,8},{8,0},{16,24},{24,16},{1,9},{9,1},{17,25},{25,17},{2,10},{10... | collective-permute-start | bytes 1179656 | tf_op jit(solution)/shard_map/ppermute | solution.py:580
  113.1 19.4 %collective-permute-start.24 = (bf16[2,128,768]{2,1,0:T(8,128)(2,1)S(1)}, bf16[2,128,768]{2,1,0:T(8,128)(2,1)S(1)}, u32[]{:S(2)}, u32[]{:S(2)}) collective-permute-start(bf16[2,128,768]{2,1,0:T(8,128)(2,1)S(1)} %get-tuple-element.285), channel_id=1, source_target_pairs={{0,16},{8,24},{16,0},{24,8},{1,17},{9,25},{17,1},{25,9},{2,18},{10... | collective-permute-start | bytes 1179656 | tf_op jit(solution)/shard_map/ppermute | solution.py:580
  113.6 18.9 %collective-permute-start.25 = (bf16[2,128,768]{2,1,0:T(8,128)(2,1)S(1)}, bf16[2,128,768]{2,1,0:T(8,128)(2,1)S(1)}, u32[]{:S(2)}, u32[]{:S(2)}) collective-permute-start(bf16[2,128,768]{2,1,0:T(8,128)(2,1)S(1)} %get-tuple-element.286), channel_id=1, source_target_pairs={{0,24},{8,16},{16,8},{24,0},{1,25},{9,17},{17,9},{25,1},{2,26},{10... | collective-permute-start | bytes 1179656 | tf_op jit(solution)/shard_map/ppermute | solution.py:580
  115.3 8.3 %collective-permute-start.20 = (bf16[1,144,768]{2,1,0:T(8,128)(2,1)S(1)}, bf16[1,144,768]{2,1,0:T(8,128)(2,1)S(1)}, u32[]{:S(2)}, u32[]{:S(2)}) collective-permute-start(bf16[1,144,768]{2,1,0:T(8,128)(2,1)S(1)} %get-tuple-element.272), channel_id=1, source_target_pairs={{0,4},{1,3},{2,6},{3,1},{4,0},{5,7},{6,2},{7,5},{8,12},{9,11},{10,... | collective-permute-start | bytes 663560 | tf_op jit(solution)/shard_map/ppermute | solution.py:599
  119.4 11.7 %collective-permute-start.26 = (bf16[1,80,768]{2,1,0:T(8,128)(2,1)S(1)}, bf16[1,80,768]{2,1,0:T(8,128)(2,1)S(1)}, u32[]{:S(2)}, u32[]{:S(2)}) collective-permute-start(bf16[1,80,768]{2,1,0:T(8,128)(2,1)S(1)} %get-tuple-element.288), channel_id=1, source_target_pairs={{0,16},{1,9},{2,18},{3,11},{4,20},{5,13},{6,22},{7,15},{8,24},{9,1... | collective-permute-start | bytes 368648 | tf_op jit(solution)/shard_map/ppermute | solution.py:590
  123.7 10.1 %collective-permute-start.22 = (bf16[1,80,768]{2,1,0:T(8,128)(2,1)S(1)}, bf16[1,80,768]{2,1,0:T(8,128)(2,1)S(1)}, u32[]{:S(2)}, u32[]{:S(2)}) collective-permute-start(bf16[1,80,768]{2,1,0:T(8,128)(2,1)S(1)} %get-tuple-element.282), channel_id=1, source_target_pairs={{0,4},{1,3},{2,6},{3,1},{4,0},{5,7},{6,2},{7,5},{8,12},{9,11},{10,... | collective-permute-start | bytes 368648 | tf_op jit(solution)/shard_map/ppermute | solution.py:599
  131.1 7.7 %collective-permute-start.27 = (bf16[144,768]{1,0:T(8,128)(2,1)S(1)}, bf16[144,768]{1,0:T(8,128)(2,1)S(1)}, u32[]{:S(2)}, u32[]{:S(2)}) collective-permute-start(bf16[144,768]{1,0:T(8,128)(2,1)S(1)} %shard_map.361.own), channel_id=1, source_target_pairs={{0,16},{1,9},{2,18},{3,11},{4,20},{5,13},{6,22},{7,15},{8,24},{9,1... | collective-permute-start | bytes 663560 | tf_op jit(solution)/shard_map/ppermute | solution.py:590
  133.8 4.9 %collective-permute-start.28 = (bf16[80,768]{1,0:T(8,128)(2,1)S(1)}, bf16[80,768]{1,0:T(8,128)(2,1)S(1)}, u32[]{:S(2)}, u32[]{:S(2)}) collective-permute-start(bf16[80,768]{1,0:T(8,128)(2,1)S(1)} %shard_map.364.own), channel_id=1, source_target_pairs={{0,16},{1,9},{2,18},{3,11},{4,20},{5,13},{6,22},{7,15},{8,24},{9,1... | collective-permute-start | bytes 368648 | tf_op jit(solution)/shard_map/ppermute | solution.py:590
  138.9 13.3 %collective-permute-start.31 = (bf16[2,144,768]{2,1,0:T(8,128)(2,1)S(1)}, bf16[2,144,768]{2,1,0:T(8,128)(2,1)S(1)}, u32[]{:S(2)}, u32[]{:S(2)}) collective-permute-start(bf16[2,144,768]{2,1,0:T(8,128)(2,1)S(1)} %shard_map.367.own), channel_id=1, source_target_pairs={{0,8},{1,17},{2,10},{3,19},{4,12},{5,21},{6,14},{7,23},{8,0},{9,25... | collective-permute-start | bytes 1327112 | tf_op jit(solution)/shard_map/ppermute | solution.py:590
  140.4 6.3 %collective-permute-start.30 = (bf16[80,768]{1,0:T(8,128)(2,1)S(1)}, bf16[80,768]{1,0:T(8,128)(2,1)S(1)}, u32[]{:S(2)}, u32[]{:S(2)}) collective-permute-start(bf16[80,768]{1,0:T(8,128)(2,1)S(1)} %shard_map.362.own), channel_id=1, source_target_pairs={{0,16},{1,9},{2,18},{3,11},{4,20},{5,13},{6,22},{7,15},{8,24},{9,1... | collective-permute-start | bytes 368648 | tf_op jit(solution)/shard_map/ppermute | solution.py:590
  141.4 8.5 %collective-permute-start.29 = (bf16[2,80,768]{2,1,0:T(8,128)(2,1)S(1)}, bf16[2,80,768]{2,1,0:T(8,128)(2,1)S(1)}, u32[]{:S(2)}, u32[]{:S(2)}) collective-permute-start(bf16[2,80,768]{2,1,0:T(8,128)(2,1)S(1)} %shard_map.365.own), channel_id=1, source_target_pairs={{0,8},{1,17},{2,10},{3,19},{4,12},{5,21},{6,14},{7,23},{8,0},{9,25... | collective-permute-start | bytes 737288 | tf_op jit(solution)/shard_map/ppermute | solution.py:590
  146.7 6.3 %collective-permute-start.32 = (bf16[2,80,768]{2,1,0:T(8,128)(2,1)S(1)}, bf16[2,80,768]{2,1,0:T(8,128)(2,1)S(1)}, u32[]{:S(2)}, u32[]{:S(2)}) collective-permute-start(bf16[2,80,768]{2,1,0:T(8,128)(2,1)S(1)} %shard_map.368.own), channel_id=1, source_target_pairs={{0,8},{1,17},{2,10},{3,19},{4,12},{5,21},{6,14},{7,23},{8,0},{9,25... | collective-permute-start | bytes 737288 | tf_op jit(solution)/shard_map/ppermute | solution.py:590
  (24 other events, 225.3 us)

commit v2 on v1

--- a/solution.py
+++ b/solution.py
@@ -470,6 +470,11 @@
     unit = down.shape[0] // 4
     down[p * unit:p * unit + DOWN_Z] = ref[j].astype(F32)
     down[p * unit + DOWN_Z:(p + 1) * unit] = tail[p]
+
+
+def last_two_kernel(up_own, up_came, down_own, down_came, up, out, down, tail):
+    last_kernel(place_up, up_own, up_came, up, out, tail)
+    last_kernel(place_down, down_own, down_came, tail, down)
 
 
 def place_rows(p, ref, j, query, key, value, vectors):
@@ -773,8 +778,10 @@
         a.gather_first()
         u.gather_first()
         d.gather_first()
-        grad_up, grad_out, tail = u.result(place_up, [(unit, ff), (unit, width), (4, unit - DOWN_Z, width)])
-        grad_down, = d.result(place_down, [(ff // PARTS, width)], tail)
+        args = order.enter(u.own.values[0], *u.came, d.own.values[0], *d.came)
+        shapes = [(unit, ff), (unit, width), (ff // PARTS, width)]
+        tail = ((4, unit - DOWN_Z, width), F32)
+        grad_up, grad_out, grad_down = call(last_two_kernel, args, [VM] * 4, [(t, F32) for t in shapes], [tail], LIMITS[6])
         grad_query, grad_key, grad_value, vectors = a.result(place_rows, [(unit, width)] * 3 + [(GROUP, width)])
         outputs, d_inputs = rows_cell.values
     else:

time: 156 us -> 155 us (level)
    pallas_call x30 -> x29, Pallas kernels: 62.3 us -> 61.7 us  [call(): pl.pallas_call(kernel, out_shape=[jax.ShapeDtypeStruct(s, d) for s, d in...]
where the time goes in v2:
time: 155 us
  Pallas kernels  61.7 us (40%)
  waiting for transfers between devices  46 us (30%)
  starting transfers between devices  40.8 us (26%)
  local copies, waits for them, and re-layouts  4.92 us (3%)
    pallas_call x29, Pallas kernels, call(): pl.pallas_call(kernel, out_shape=[jax.ShapeDtypeStruct(s, d) for s, d in...  61.7 us
    ppermute x12, waiting for transfers between devices, swap_first(): return lax.ppermute(array, ('blk', 'batch'), perm)  31.7 us
    ppermute x6, starting transfers between devices, swap_z(): lax.ppermute(array, 'batch', [(i, i ^ (2 if (i % 2 == 0) == first else 4)...  14.6 us
    ppermute x12, starting transfers between devices, swap_first(): return lax.ppermute(array, ('blk', 'batch'), perm)  12.7 us
    ppermute x9, starting transfers between devices, swap(): lax.ppermute(array, 'blk', [(i, i ^ bit) for i in range(lax.axis_size('bl...  11.7 us
    ppermute x6, waiting for transfers between devices, swap_z(): lax.ppermute(array, 'batch', [(i, i ^ (2 if (i % 2 == 0) == first else 4)...  9.16 us
    ppermute x6, waiting for transfers between devices, swap_batch(): lax.ppermute(array, 'batch', [(i, i ^ bit) for i in range(lax.axis_size('...  5.08 us
  transfers between devices with their start and end apart: 33, of which 16 were waited for; matrix products, arithmetic and copies ran while one was open for 1% of the time, Pallas kernels for 26%

profile of v2, /device:TPU:0, one launch (start us, length us, event | category | flops | bytes accessed | tf_op | source)
XLA Modules:
  0.0 154.7 jit_solution(905482178825987420)
XLA Ops:
  2.0 3.0 %collective-permute-start = (bf16[128,768]{1,0:T(8,128)(2,1)S(1)}, bf16[128,768]{1,0:T(8,128)(2,1)S(1)}, u32[]{:S(2)}, u32[]{:S(2)}) collective-permute-start(bf16[128,768]{1,0:T(8,128)(2,1)S(1)} %get-tuple-element.330), channel_id=1, source_target_pairs={{0,8},{8,0},{16,24},{24,16},{1,9},{9,1},{17,25},{25,17},{2,10},{10... | collective-permute-start | bytes 589832 | tf_op jit(solution)/shard_map/ppermute | solution.py:585
  8.9 3.8 %shard_map.341 = (bf16[512,768]{1,0:T(8,128)(2,1)S(1)}, f32[512,128]{1,0:T(8,128)S(1)}) custom-call(s32[4,80]{1,0:T(4,128)S(1)} %copy-done.9, s32[4]{0:T(128)S(1)} %copy-done.18, s32[4,80]{1,0:T(4,128)S(1)} %copy-done.10, bf16[15360,768]{1,0:T(8,128)(2,1)} %table_ref.1), custom_call_target="tpu_custom_call" | custom-call | flops 1024 | bytes 1024 | tf_op jit(solution)/shard_map/pallas_call | solution.py:508
  12.7 1.9 %collective-permute-start.3 = (bf16[128,768]{1,0:T(8,128)(2,1)S(1)}, bf16[128,768]{1,0:T(8,128)(2,1)S(1)}, u32[]{:S(2)}, u32[]{:S(2)}) collective-permute-start(bf16[128,768]{1,0:T(8,128)(2,1)S(1)} %get-tuple-element.327), channel_id=1, source_target_pairs={{0,8},{8,0},{16,24},{24,16},{1,9},{9,1},{17,25},{25,17},{2,10},{10... | collective-permute-start | bytes 589832 | tf_op jit(solution)/shard_map/ppermute | solution.py:585
  14.6 1.5 collective-permute-start.4
  16.4 9.4 %shard_map.342 = (bf16[768,512]{1,0:T(8,128)(2,1)S(1)}, bf16[512,768]{1,0:T(8,128)(2,1)S(1)}, bf16[512,768]{1,0:T(8,128)(2,1)S(1)}, bf16[512,768]{1,0:T(8,128)(2...) custom-call(s32[4]{0:T(128)S(1)} %copy-done.8, ...), custom_call_target="tpu_custom_call" | custom-call | flops 1024 | bytes 1024 | tf_op jit(solution)/shard_map/pallas_call | solution.py:508
  26.0 19.3 %shard_map.343 = (bf16[512,768]{1,0:T(8,128)(2,1)S(1)}, bf16[4,4,80,768]{3,2,1,0:T(8,128)(2,1)S(1)}, bf16[4,4,80,768]{3,2,1,0:T(8,128)(2,1)S(1)}, bf16[4,4,112,7...) custom-call(f32[512,768]{1,0:T(8,128)S(1)} %get-tuple-element.174.n_, ...), custom_call_target="tpu_custom_call" | custom-call | flops 1024 | bytes 1024 | tf_op jit(solution)/shard_map/pallas_call | solution.py:508
  45.9 5.0 %shard_map.344 = (bf16[4,4,32,768]{3,2,1,0:T(8,128)(2,1)S(1)}, bf16[4,4,32,768]{3,2,1,0:T(8,128)(2,1)S(1)}, f32[512,768]{1,0:T(8,128)S(1)}, bf16[512,768]{1,0:T(8,128)(2,1)S(1)}, f32[16,768]{1,0:T(8,128)S(1)}) custom-call(f32[512,768]{1,0:T(8,128)S(1)} %get-tuple-element.174.n_ref, f32[512,128]{1,0:T(8,128)S(1)} %get-tuple-element.179.rstd_ref, ...), custom_call_target="tpu_custom_call" | custom-call | flops 1024 | bytes 1024 | tf_op jit(solution)/shard_map/pallas_call | solution.py:508
  55.3 1.9 %collective-permute-start.9 = (bf16[8,144,768]{2,1,0:T(8,128)(2,1)S(1)}, bf16[8,144,768]{2,1,0:T(8,128)(2,1)S(1)}, u32[]{:S(2)}, u32[]{:S(2)}) collective-permute-start(bf16[8,144,768]{2,1,0:T(8,128)(2,1)S(1)} %get-tuple-element.203), channel_id=1, source_target_pairs={{0,8},{1,17},{2,10},{3,19},{4,12},{5,21},{6,14},{7,23},{8,0},{9,25... | collective-permute-start | bytes 5308424 | tf_op jit(solution)/shard_map/ppermute | solution.py:595
  57.2 1.6 %collective-permute-start.10 = (bf16[8,80,768]{2,1,0:T(8,128)(2,1)S(1)}, bf16[8,80,768]{2,1,0:T(8,128)(2,1)S(1)}, u32[]{:S(2)}, u32[]{:S(2)}) collective-permute-start(bf16[8,80,768]{2,1,0:T(8,128)(2,1)S(1)} %get-tuple-element.205), channel_id=1, source_target_pairs={{0,2},{1,5},{2,0},{3,7},{4,6},{5,1},{6,4},{7,3},{8,10},{9,13},{10,... | collective-permute-start | bytes 2949128 | tf_op jit(solution)/shard_map/ppermute | solution.py:604
  58.7 8.8 %shard_map.348 = (bf16[512,512]{1,0:T(8,128)(2,1)S(1)}, bf16[512,512]{1,0:T(8,128)(2,1)S(1)}, bf16[512,512]{1,0:T(8,128)(2,1)S(1)}, bf16[4,4,80,512]{3,2,1,0:T(8...) custom-call(s32[4]{0:T(128)S(1)} %copy-done.8, ...), custom_call_target="tpu_custom_call" | custom-call | flops 1024 | bytes 1024 | tf_op jit(solution)/shard_map/pallas_call | solution.py:508
  67.5 4.8 %shard_map.349 = (bf16[512,256]{1,0:T(8,128)(2,1)S(1)}, bf16[512,256]{1,0:T(8,128)(2,1)S(1)}, bf16[512,256]{1,0:T(8,128)(2,1)S(1)}, bf16[4,4,80,256]{3,2,1,0:T(8,128)(2,1)S(1)}, bf16[4,4,80,256]{3,2,1,0:T(8,128)(2,1)S(1)}) custom-call(s32[4]{0:T(128)S(1)} %copy-done.8, bf16[768,512]{1,0:T(8,128)(2,1)S(1)} %get-tuple-element.206.x_t_ref, ...), custom_call_target="tpu_custom_call" | custom-call | flops 1024 | bytes 1024 | tf_op jit(solution)/shard_map/pallas_call | solution.py:508
  77.1 1.5 collective-permute-start.15
  78.6 2.9 %collective-permute-done.10 = bf16[8,80,768]{2,1,0:T(8,128)(2,1)S(1)} collective-permute-done((bf16[8,80,768]{2,1,0:T(8,128)(2,1)S(1)}, bf16[8,80,768]{2,1,0:T(8,128)(2,1)S(1)}, u32[]{:S(2)}, u32[]{:S(2)}) %collective-permute-start.10) | collective-permute-done | bytes 983072 | tf_op jit(solution)/shard_map/ppermute | solution.py:604
  82.3 3.3 %collective-permute-start.17 = (bf16[4,80,768]{2,1,0:T(8,128)(2,1)S(1)}, bf16[4,80,768]{2,1,0:T(8,128)(2,1)S(1)}, u32[]{:S(2)}, u32[]{:S(2)}) collective-permute-start(bf16[4,80,768]{2,1,0:T(8,128)(2,1)S(1)} %get-tuple-element.253), channel_id=1, source_target_pairs={{0,4},{1,3},{2,6},{3,1},{4,0},{5,7},{6,2},{7,5},{8,12},{9,11},{10,... | collective-permute-start | bytes 1474568 | tf_op jit(solution)/shard_map/ppermute | solution.py:604
  85.6 2.1 %shard_map.353 = (bf16[512,768]{1,0:T(8,128)(2,1)S(1)}, bf16[2,128,768]{2,1,0:T(8,128)(2,1)S(1)}, bf16[2,128,768]{2,1,0:T(8,128)(2,1)S(1)}, bf16[2,128,768]{2,1,0:T(8,128)(2,1)S(1)}) custom-call(f32[512,128]{1,0:T(8,128)S(1)} %get-tuple-element.237.hit_ref, bf16[512,768]{1,0:T(8,128)(2,1)S(1)} %get-tuple-element.238.out_page, ...), custom_call_target="tpu_custom_call" | custom-call | flops 1024 | bytes 1024 | tf_op jit(solution)/shard_map/pallas_call | solution.py:508
  87.8 9.9 %collective-permute-done.15 = bf16[8,80,768]{2,1,0:T(8,128)(2,1)S(1)} collective-permute-done((bf16[8,80,768]{2,1,0:T(8,128)(2,1)S(1)}, bf16[8,80,768]{2,1,0:T(8,128)(2,1)S(1)}, u32[]{:S(2)}, u32[]{:S(2)}) %collective-permute-start.15) | collective-permute-done | bytes 983072 | tf_op jit(solution)/shard_map/ppermute | solution.py:595
  97.9 1.9 %collective-permute-start.16 = (bf16[4,80,768]{2,1,0:T(8,128)(2,1)S(1)}, bf16[4,80,768]{2,1,0:T(8,128)(2,1)S(1)}, u32[]{:S(2)}, u32[]{:S(2)}) collective-permute-start(bf16[4,80,768]{2,1,0:T(8,128)(2,1)S(1)} %get-tuple-element.251), channel_id=1, source_target_pairs={{0,16},{1,9},{2,18},{3,11},{4,20},{5,13},{6,22},{7,15},{8,24},{9,1... | collective-permute-start | bytes 1474568 | tf_op jit(solution)/shard_map/ppermute | solution.py:595
  100.4 1.6 %collective-permute-start.19 = (bf16[2,144,768]{2,1,0:T(8,128)(2,1)S(1)}, bf16[2,144,768]{2,1,0:T(8,128)(2,1)S(1)}, u32[]{:S(2)}, u32[]{:S(2)}) collective-permute-start(bf16[2,144,768]{2,1,0:T(8,128)(2,1)S(1)} %get-tuple-element.263), channel_id=1, source_target_pairs={{0,2},{1,5},{2,0},{3,7},{4,6},{5,1},{6,4},{7,3},{8,10},{9,13},{10,... | collective-permute-start | bytes 1327112 | tf_op jit(solution)/shard_map/ppermute | solution.py:604
  102.1 1.5 collective-permute-start.18
  103.7 4.1 %collective-permute-done.16 = bf16[4,80,768]{2,1,0:T(8,128)(2,1)S(1)} collective-permute-done((bf16[4,80,768]{2,1,0:T(8,128)(2,1)S(1)}, bf16[4,80,768]{2,1,0:T(8,128)(2,1)S(1)}, u32[]{:S(2)}, u32[]{:S(2)}) %collective-permute-start.16) | collective-permute-done | bytes 491552 | tf_op jit(solution)/shard_map/ppermute | solution.py:595
  108.0 3.7 %collective-permute-start.21 = (bf16[2,80,768]{2,1,0:T(8,128)(2,1)S(1)}, bf16[2,80,768]{2,1,0:T(8,128)(2,1)S(1)}, u32[]{:S(2)}, u32[]{:S(2)}) collective-permute-start(bf16[2,80,768]{2,1,0:T(8,128)(2,1)S(1)} %get-tuple-element.273), channel_id=1, source_target_pairs={{0,2},{1,5},{2,0},{3,7},{4,6},{5,1},{6,4},{7,3},{8,10},{9,13},{10,... | collective-permute-start | bytes 737288 | tf_op jit(solution)/shard_map/ppermute | solution.py:604
  113.6 1.6 %collective-permute-start.25 = (bf16[2,128,768]{2,1,0:T(8,128)(2,1)S(1)}, bf16[2,128,768]{2,1,0:T(8,128)(2,1)S(1)}, u32[]{:S(2)}, u32[]{:S(2)}) collective-permute-start(bf16[2,128,768]{2,1,0:T(8,128)(2,1)S(1)} %get-tuple-element.285), channel_id=1, source_target_pairs={{0,24},{8,16},{16,8},{24,0},{1,25},{9,17},{17,9},{25,1},{2,26},{10... | collective-permute-start | bytes 1179656 | tf_op jit(solution)/shard_map/ppermute | solution.py:585
  115.3 1.9 %collective-permute-start.20 = (bf16[1,144,768]{2,1,0:T(8,128)(2,1)S(1)}, bf16[1,144,768]{2,1,0:T(8,128)(2,1)S(1)}, u32[]{:S(2)}, u32[]{:S(2)}) collective-permute-start(bf16[1,144,768]{2,1,0:T(8,128)(2,1)S(1)} %get-tuple-element.271), channel_id=1, source_target_pairs={{0,4},{1,3},{2,6},{3,1},{4,0},{5,7},{6,2},{7,5},{8,12},{9,11},{10,... | collective-permute-start | bytes 663560 | tf_op jit(solution)/shard_map/ppermute | solution.py:604
  117.3 2.1 %collective-permute-done.21 = bf16[2,80,768]{2,1,0:T(8,128)(2,1)S(1)} collective-permute-done((bf16[2,80,768]{2,1,0:T(8,128)(2,1)S(1)}, bf16[2,80,768]{2,1,0:T(8,128)(2,1)S(1)}, u32[]{:S(2)}, u32[]{:S(2)}) %collective-permute-start.21) | collective-permute-done | bytes 245792 | tf_op jit(solution)/shard_map/ppermute | solution.py:604
  119.5 4.2 %collective-permute-done.20.came = bf16[1,144,768]{2,1,0:T(8,128)(2,1)S(1)} collective-permute-done((bf16[1,144,768]{2,1,0:T(8,128)(2,1)S(1)}, bf16[1,144,768]{2,1,0:T(8,128)(2,1)S(1)}, u32[]{:S(2)}, u32[]{:S(2)}) %collective-permute-start.20) | collective-permute-done | bytes 221216 | tf_op jit(solution)/shard_map/ppermute | solution.py:604
  123.7 2.4 %collective-permute-start.22 = (bf16[1,80,768]{2,1,0:T(8,128)(2,1)S(1)}, bf16[1,80,768]{2,1,0:T(8,128)(2,1)S(1)}, u32[]{:S(2)}, u32[]{:S(2)}) collective-permute-start(bf16[1,80,768]{2,1,0:T(8,128)(2,1)S(1)} %get-tuple-element.281), channel_id=1, source_target_pairs={{0,4},{1,3},{2,6},{3,1},{4,0},{5,7},{6,2},{7,5},{8,12},{9,11},{10,... | collective-permute-start | bytes 368648 | tf_op jit(solution)/shard_map/ppermute | solution.py:604
  126.1 5.0 %collective-permute-done.26.came = bf16[1,80,768]{2,1,0:T(8,128)(2,1)S(1)} collective-permute-done((bf16[1,80,768]{2,1,0:T(8,128)(2,1)S(1)}, bf16[1,80,768]{2,1,0:T(8,128)(2,1)S(1)}, u32[]{:S(2)}, u32[]{:S(2)}) %collective-permute-start.26) | collective-permute-done | bytes 122912 | tf_op jit(solution)/shard_map/ppermute | solution.py:595
  134.6 4.2 %collective-permute-done.28.came = bf16[80,768]{1,0:T(8,128)(2,1)S(1)} collective-permute-done((bf16[80,768]{1,0:T(8,128)(2,1)S(1)}, bf16[80,768]{1,0:T(8,128)(2,1)S(1)}, u32[]{:S(2)}, u32[]{:S(2)}) %collective-permute-start.28) | collective-permute-done | bytes 122912 | tf_op jit(solution)/shard_map/ppermute | solution.py:595
  138.9 1.6 %collective-permute-start.31 = (bf16[2,144,768]{2,1,0:T(8,128)(2,1)S(1)}, bf16[2,144,768]{2,1,0:T(8,128)(2,1)S(1)}, u32[]{:S(2)}, u32[]{:S(2)}) collective-permute-start(bf16[2,144,768]{2,1,0:T(8,128)(2,1)S(1)} %shard_map.367.up_own), channel_id=1, source_target_pairs={{0,8},{1,17},{2,10},{3,19},{4,12},{5,21},{6,14},{7,23},{8,0},{9,25... | collective-permute-start | bytes 1327112 | tf_op jit(solution)/shard_map/ppermute | solution.py:595
  141.9 4.8 %collective-permute-done.30.came = bf16[80,768]{1,0:T(8,128)(2,1)S(1)} collective-permute-done((bf16[80,768]{1,0:T(8,128)(2,1)S(1)}, bf16[80,768]{1,0:T(8,128)(2,1)S(1)}, u32[]{:S(2)}, u32[]{:S(2)}) %collective-permute-start.30) | collective-permute-done | bytes 122912 | tf_op jit(solution)/shard_map/ppermute | solution.py:595
  147.3 2.6 %collective-permute-done.29.came = bf16[2,80,768]{2,1,0:T(8,128)(2,1)S(1)} collective-permute-done((bf16[2,80,768]{2,1,0:T(8,128)(2,1)S(1)}, bf16[2,80,768]{2,1,0:T(8,128)(2,1)S(1)}, u32[]{:S(2)}, u32[]{:S(2)}) %collective-permute-start.29) | collective-permute-done | bytes 245792 | tf_op jit(solution)/shard_map/ppermute | solution.py:595
  153.0 1.7 %shard_map.369 = (f32[96,3072]{1,0:T(8,128)}, f32[96,768]{1,0:T(8,128)}, f32[384,768]{1,0:T(8,128)}) custom-call(bf16[2,144,768]{2,1,0:T(8,128)(2,1)S(1)} %shard_map.367.up_own, bf16[2,144,768]{2,1,0:T(8,128)(2,1)S(1)} %collective-permute-done.31.up_came, bf16[2,80,768]{2,1,0:T(8,128)(2,1)S(1)} %shard_map.368.down_own, ...), custom_call_target="tpu_custom_call" | custom-call | flops 1024 | bytes 1024 | tf_op jit(solution)/shard_map/pallas_call | solution.py:508
  (117 shorter events, 28.0 us)
Async XLA Ops:
  2.0 14.1 %collective-permute-start = (bf16[128,768]{1,0:T(8,128)(2,1)S(1)}, bf16[128,768]{1,0:T(8,128)(2,1)S(1)}, u32[]{:S(2)}, u32[]{:S(2)}) collective-permute-start(bf16[128,768]{1,0:T(8,128)(2,1)S(1)} %get-tuple-element.330), channel_id=1, source_target_pairs={{0,8},{8,0},{16,24},{24,16},{1,9},{9,1},{17,25},{25,17},{2,10},{10... | collective-permute-start | bytes 589832 | tf_op jit(solution)/shard_map/ppermute | solution.py:585
  5.0 11.2 %collective-permute-start.1 = (bf16[128,768]{1,0:T(8,128)(2,1)S(1)}, bf16[128,768]{1,0:T(8,128)(2,1)S(1)}, u32[]{:S(2)}, u32[]{:S(2)}) collective-permute-start(bf16[128,768]{1,0:T(8,128)(2,1)S(1)} %get-tuple-element.329), channel_id=1, source_target_pairs={{0,16},{8,24},{16,0},{24,8},{1,17},{9,25},{17,1},{25,9},{2,18},{10... | collective-permute-start | bytes 589832 | tf_op jit(solution)/shard_map/ppermute | solution.py:585
  6.6 9.7 %collective-permute-start.2 = (bf16[128,768]{1,0:T(8,128)(2,1)S(1)}, bf16[128,768]{1,0:T(8,128)(2,1)S(1)}, u32[]{:S(2)}, u32[]{:S(2)}) collective-permute-start(bf16[128,768]{1,0:T(8,128)(2,1)S(1)} %get-tuple-element.328), channel_id=1, source_target_pairs={{0,24},{8,16},{16,8},{24,0},{1,25},{9,17},{17,9},{25,1},{2,26},{10... | collective-permute-start | bytes 589832 | tf_op jit(solution)/shard_map/ppermute | solution.py:585
  12.7 13.2 %collective-permute-start.3 = (bf16[128,768]{1,0:T(8,128)(2,1)S(1)}, bf16[128,768]{1,0:T(8,128)(2,1)S(1)}, u32[]{:S(2)}, u32[]{:S(2)}) collective-permute-start(bf16[128,768]{1,0:T(8,128)(2,1)S(1)} %get-tuple-element.327), channel_id=1, source_target_pairs={{0,8},{8,0},{16,24},{24,16},{1,9},{9,1},{17,25},{25,17},{2,10},{10... | collective-permute-start | bytes 589832 | tf_op jit(solution)/shard_map/ppermute | solution.py:585
  14.6 11.3 %collective-permute-start.4 = (bf16[128,768]{1,0:T(8,128)(2,1)S(1)}, bf16[128,768]{1,0:T(8,128)(2,1)S(1)}, u32[]{:S(2)}, u32[]{:S(2)}) collective-permute-start(bf16[128,768]{1,0:T(8,128)(2,1)S(1)} %get-tuple-element.326), channel_id=1, source_target_pairs={{0,16},{8,24},{16,0},{24,8},{1,17},{9,25},{17,1},{25,9},{2,18},{10... | collective-permute-start | bytes 589832 | tf_op jit(solution)/shard_map/ppermute | solution.py:585
  16.1 9.8 %collective-permute-start.5 = (bf16[128,768]{1,0:T(8,128)(2,1)S(1)}, bf16[128,768]{1,0:T(8,128)(2,1)S(1)}, u32[]{:S(2)}, u32[]{:S(2)}) collective-permute-start(bf16[128,768]{1,0:T(8,128)(2,1)S(1)} %get-tuple-element.325), channel_id=1, source_target_pairs={{0,24},{8,16},{16,8},{24,0},{1,25},{9,17},{17,9},{25,1},{2,26},{10... | collective-permute-start | bytes 589832 | tf_op jit(solution)/shard_map/ppermute | solution.py:585
  45.3 9.1 %collective-permute-start.7 = (bf16[4,4,112,768]{3,2,1,0:T(8,128)(2,1)S(1)}, bf16[4,4,112,768]{3,2,1,0:T(8,128)(2,1)S(1)}, u32[]{:S(2)}, u32[]{:S(2)}) collective-permute-start(bf16[4,4,112,768]{3,2,1,0:T(8,128)(2,1)S(1)} %get-tuple-element.192), channel_id=1, source_target_pairs={{0,1},{1,0},{2,3},{3,2},{4,5},{5,4},{6,7},{7,6},{8,9},{9,8},{10,11... | collective-permute-start | bytes 8257544 | tf_op jit(solution)/shard_map/ppermute | solution.py:599
  45.4 7.9 %collective-permute-start.6 = (bf16[4,4,80,768]{3,2,1,0:T(8,128)(2,1)S(1)}, bf16[4,4,80,768]{3,2,1,0:T(8,128)(2,1)S(1)}, u32[]{:S(2)}, u32[]{:S(2)}) collective-permute-start(bf16[4,4,80,768]{3,2,1,0:T(8,128)(2,1)S(1)} %get-tuple-element.177), channel_id=1, source_target_pairs={{0,1},{1,0},{2,3},{3,2},{4,5},{5,4},{6,7},{7,6},{8,9},{9,8},{10,11... | collective-permute-start | bytes 5898248 | tf_op jit(solution)/shard_map/ppermute | solution.py:599
  50.9 3.5 %collective-permute-start.8 = (bf16[4,4,32,768]{3,2,1,0:T(8,128)(2,1)S(1)}, bf16[4,4,32,768]{3,2,1,0:T(8,128)(2,1)S(1)}, u32[]{:S(2)}, u32[]{:S(2)}) collective-permute-start(bf16[4,4,32,768]{3,2,1,0:T(8,128)(2,1)S(1)} %get-tuple-element.193), channel_id=1, source_target_pairs={{0,1},{1,0},{2,3},{3,2},{4,5},{5,4},{6,7},{7,6},{8,9},{9,8},{10,11... | collective-permute-start | bytes 2359304 | tf_op jit(solution)/shard_map/ppermute | solution.py:599
  55.3 26.5 %collective-permute-start.9 = (bf16[8,144,768]{2,1,0:T(8,128)(2,1)S(1)}, bf16[8,144,768]{2,1,0:T(8,128)(2,1)S(1)}, u32[]{:S(2)}, u32[]{:S(2)}) collective-permute-start(bf16[8,144,768]{2,1,0:T(8,128)(2,1)S(1)} %get-tuple-element.203), channel_id=1, source_target_pairs={{0,8},{1,17},{2,10},{3,19},{4,12},{5,21},{6,14},{7,23},{8,0},{9,25... | collective-permute-start | bytes 5308424 | tf_op jit(solution)/shard_map/ppermute | solution.py:595
  57.2 24.3 %collective-permute-start.10 = (bf16[8,80,768]{2,1,0:T(8,128)(2,1)S(1)}, bf16[8,80,768]{2,1,0:T(8,128)(2,1)S(1)}, u32[]{:S(2)}, u32[]{:S(2)}) collective-permute-start(bf16[8,80,768]{2,1,0:T(8,128)(2,1)S(1)} %get-tuple-element.205), channel_id=1, source_target_pairs={{0,2},{1,5},{2,0},{3,7},{4,6},{5,1},{6,4},{7,3},{8,10},{9,13},{10,... | collective-permute-start | bytes 2949128 | tf_op jit(solution)/shard_map/ppermute | solution.py:604
  73.0 2.7 %collective-permute-start.11 = (bf16[2,4,80,512]{3,2,1,0:T(8,128)(2,1)S(1)}, bf16[2,4,80,512]{3,2,1,0:T(8,128)(2,1)S(1)}, u32[]{:S(2)}, u32[]{:S(2)}) collective-permute-start(bf16[2,4,80,512]{3,2,1,0:T(8,128)(2,1)S(1)} %get-tuple-element.218), channel_id=1, source_target_pairs={{0,1},{1,0},{2,3},{3,2},{4,5},{5,4},{6,7},{7,6},{8,9},{9,8},{10,11... | collective-permute-start | bytes 1966088 | tf_op jit(solution)/shard_map/ppermute | solution.py:599
  73.1 3.5 %collective-permute-start.12 = (bf16[2,4,80,512]{3,2,1,0:T(8,128)(2,1)S(1)}, bf16[2,4,80,512]{3,2,1,0:T(8,128)(2,1)S(1)}, u32[]{:S(2)}, u32[]{:S(2)}) collective-permute-start(bf16[2,4,80,512]{3,2,1,0:T(8,128)(2,1)S(1)} %get-tuple-element.219), channel_id=1, source_target_pairs={{0,1},{1,0},{2,3},{3,2},{4,5},{5,4},{6,7},{7,6},{8,9},{9,8},{10,11... | collective-permute-start | bytes 1966088 | tf_op jit(solution)/shard_map/ppermute | solution.py:599
  77.1 20.6 %collective-permute-start.15 = (bf16[8,80,768]{2,1,0:T(8,128)(2,1)S(1)}, bf16[8,80,768]{2,1,0:T(8,128)(2,1)S(1)}, u32[]{:S(2)}, u32[]{:S(2)}) collective-permute-start(bf16[8,80,768]{2,1,0:T(8,128)(2,1)S(1)} %get-tuple-element.236), channel_id=1, source_target_pairs={{0,8},{1,17},{2,10},{3,19},{4,12},{5,21},{6,14},{7,23},{8,0},{9,25... | collective-permute-start | bytes 2949128 | tf_op jit(solution)/shard_map/ppermute | solution.py:595
  82.2 17.9 %collective-permute-start.14 = (bf16[4,144,768]{2,1,0:T(8,128)(2,1)S(1)}, bf16[4,144,768]{2,1,0:T(8,128)(2,1)S(1)}, u32[]{:S(2)}, u32[]{:S(2)}) collective-permute-start(bf16[4,144,768]{2,1,0:T(8,128)(2,1)S(1)} %get-tuple-element.234), channel_id=1, source_target_pairs={{0,16},{1,9},{2,18},{3,11},{4,20},{5,13},{6,22},{7,15},{8,24},{9,1... | collective-permute-start | bytes 2654216 | tf_op jit(solution)/shard_map/ppermute | solution.py:595
  82.3 19.7 %collective-permute-start.17 = (bf16[4,80,768]{2,1,0:T(8,128)(2,1)S(1)}, bf16[4,80,768]{2,1,0:T(8,128)(2,1)S(1)}, u32[]{:S(2)}, u32[]{:S(2)}) collective-permute-start(bf16[4,80,768]{2,1,0:T(8,128)(2,1)S(1)} %get-tuple-element.253), channel_id=1, source_target_pairs={{0,4},{1,3},{2,6},{3,1},{4,0},{5,7},{6,2},{7,5},{8,12},{9,11},{10,... | collective-permute-start | bytes 1474568 | tf_op jit(solution)/shard_map/ppermute | solution.py:604
  97.9 9.9 %collective-permute-start.16 = (bf16[4,80,768]{2,1,0:T(8,128)(2,1)S(1)}, bf16[4,80,768]{2,1,0:T(8,128)(2,1)S(1)}, u32[]{:S(2)}, u32[]{:S(2)}) collective-permute-start(bf16[4,80,768]{2,1,0:T(8,128)(2,1)S(1)} %get-tuple-element.251), channel_id=1, source_target_pairs={{0,16},{1,9},{2,18},{3,11},{4,20},{5,13},{6,22},{7,15},{8,24},{9,1... | collective-permute-start | bytes 1474568 | tf_op jit(solution)/shard_map/ppermute | solution.py:595
  100.4 13.2 %collective-permute-start.19 = (bf16[2,144,768]{2,1,0:T(8,128)(2,1)S(1)}, bf16[2,144,768]{2,1,0:T(8,128)(2,1)S(1)}, u32[]{:S(2)}, u32[]{:S(2)}) collective-permute-start(bf16[2,144,768]{2,1,0:T(8,128)(2,1)S(1)} %get-tuple-element.263), channel_id=1, source_target_pairs={{0,2},{1,5},{2,0},{3,7},{4,6},{5,1},{6,4},{7,3},{8,10},{9,13},{10,... | collective-permute-start | bytes 1327112 | tf_op jit(solution)/shard_map/ppermute | solution.py:604
  102.1 13.2 %collective-permute-start.18 = (bf16[2,80,768]{2,1,0:T(8,128)(2,1)S(1)}, bf16[2,80,768]{2,1,0:T(8,128)(2,1)S(1)}, u32[]{:S(2)}, u32[]{:S(2)}) collective-permute-start(bf16[2,80,768]{2,1,0:T(8,128)(2,1)S(1)} %get-tuple-element.261), channel_id=1, source_target_pairs={{0,8},{1,17},{2,10},{3,19},{4,12},{5,21},{6,14},{7,23},{8,0},{9,25... | collective-permute-start | bytes 737288 | tf_op jit(solution)/shard_map/ppermute | solution.py:595
  108.0 11.5 %collective-permute-start.21 = (bf16[2,80,768]{2,1,0:T(8,128)(2,1)S(1)}, bf16[2,80,768]{2,1,0:T(8,128)(2,1)S(1)}, u32[]{:S(2)}, u32[]{:S(2)}) collective-permute-start(bf16[2,80,768]{2,1,0:T(8,128)(2,1)S(1)} %get-tuple-element.273), channel_id=1, source_target_pairs={{0,2},{1,5},{2,0},{3,7},{4,6},{5,1},{6,4},{7,3},{8,10},{9,13},{10,... | collective-permute-start | bytes 737288 | tf_op jit(solution)/shard_map/ppermute | solution.py:604
  111.7 20.8 %collective-permute-start.23 = (bf16[2,128,768]{2,1,0:T(8,128)(2,1)S(1)}, bf16[2,128,768]{2,1,0:T(8,128)(2,1)S(1)}, u32[]{:S(2)}, u32[]{:S(2)}) collective-permute-start(bf16[2,128,768]{2,1,0:T(8,128)(2,1)S(1)} %get-tuple-element.283), channel_id=1, source_target_pairs={{0,8},{8,0},{16,24},{24,16},{1,9},{9,1},{17,25},{25,17},{2,10},{10... | collective-permute-start | bytes 1179656 | tf_op jit(solution)/shard_map/ppermute | solution.py:585
  113.1 19.4 %collective-permute-start.24 = (bf16[2,128,768]{2,1,0:T(8,128)(2,1)S(1)}, bf16[2,128,768]{2,1,0:T(8,128)(2,1)S(1)}, u32[]{:S(2)}, u32[]{:S(2)}) collective-permute-start(bf16[2,128,768]{2,1,0:T(8,128)(2,1)S(1)} %get-tuple-element.284), channel_id=1, source_target_pairs={{0,16},{8,24},{16,0},{24,8},{1,17},{9,25},{17,1},{25,9},{2,18},{10... | collective-permute-start | bytes 1179656 | tf_op jit(solution)/shard_map/ppermute | solution.py:585
  113.6 18.9 %collective-permute-start.25 = (bf16[2,128,768]{2,1,0:T(8,128)(2,1)S(1)}, bf16[2,128,768]{2,1,0:T(8,128)(2,1)S(1)}, u32[]{:S(2)}, u32[]{:S(2)}) collective-permute-start(bf16[2,128,768]{2,1,0:T(8,128)(2,1)S(1)} %get-tuple-element.285), channel_id=1, source_target_pairs={{0,24},{8,16},{16,8},{24,0},{1,25},{9,17},{17,9},{25,1},{2,26},{10... | collective-permute-start | bytes 1179656 | tf_op jit(solution)/shard_map/ppermute | solution.py:585
  115.3 8.3 %collective-permute-start.20 = (bf16[1,144,768]{2,1,0:T(8,128)(2,1)S(1)}, bf16[1,144,768]{2,1,0:T(8,128)(2,1)S(1)}, u32[]{:S(2)}, u32[]{:S(2)}) collective-permute-start(bf16[1,144,768]{2,1,0:T(8,128)(2,1)S(1)} %get-tuple-element.271), channel_id=1, source_target_pairs={{0,4},{1,3},{2,6},{3,1},{4,0},{5,7},{6,2},{7,5},{8,12},{9,11},{10,... | collective-permute-start | bytes 663560 | tf_op jit(solution)/shard_map/ppermute | solution.py:604
  119.4 11.7 %collective-permute-start.26 = (bf16[1,80,768]{2,1,0:T(8,128)(2,1)S(1)}, bf16[1,80,768]{2,1,0:T(8,128)(2,1)S(1)}, u32[]{:S(2)}, u32[]{:S(2)}) collective-permute-start(bf16[1,80,768]{2,1,0:T(8,128)(2,1)S(1)} %get-tuple-element.287), channel_id=1, source_target_pairs={{0,16},{1,9},{2,18},{3,11},{4,20},{5,13},{6,22},{7,15},{8,24},{9,1... | collective-permute-start | bytes 368648 | tf_op jit(solution)/shard_map/ppermute | solution.py:595
  123.7 10.1 %collective-permute-start.22 = (bf16[1,80,768]{2,1,0:T(8,128)(2,1)S(1)}, bf16[1,80,768]{2,1,0:T(8,128)(2,1)S(1)}, u32[]{:S(2)}, u32[]{:S(2)}) collective-permute-start(bf16[1,80,768]{2,1,0:T(8,128)(2,1)S(1)} %get-tuple-element.281), channel_id=1, source_target_pairs={{0,4},{1,3},{2,6},{3,1},{4,0},{5,7},{6,2},{7,5},{8,12},{9,11},{10,... | collective-permute-start | bytes 368648 | tf_op jit(solution)/shard_map/ppermute | solution.py:604
  131.1 7.7 %collective-permute-start.27 = (bf16[144,768]{1,0:T(8,128)(2,1)S(1)}, bf16[144,768]{1,0:T(8,128)(2,1)S(1)}, u32[]{:S(2)}, u32[]{:S(2)}) collective-permute-start(bf16[144,768]{1,0:T(8,128)(2,1)S(1)} %shard_map.361.own), channel_id=1, source_target_pairs={{0,16},{1,9},{2,18},{3,11},{4,20},{5,13},{6,22},{7,15},{8,24},{9,1... | collective-permute-start | bytes 663560 | tf_op jit(solution)/shard_map/ppermute | solution.py:595
  133.8 4.9 %collective-permute-start.28 = (bf16[80,768]{1,0:T(8,128)(2,1)S(1)}, bf16[80,768]{1,0:T(8,128)(2,1)S(1)}, u32[]{:S(2)}, u32[]{:S(2)}) collective-permute-start(bf16[80,768]{1,0:T(8,128)(2,1)S(1)} %shard_map.364.own), channel_id=1, source_target_pairs={{0,16},{1,9},{2,18},{3,11},{4,20},{5,13},{6,22},{7,15},{8,24},{9,1... | collective-permute-start | bytes 368648 | tf_op jit(solution)/shard_map/ppermute | solution.py:595
  138.9 14.1 %collective-permute-start.31 = (bf16[2,144,768]{2,1,0:T(8,128)(2,1)S(1)}, bf16[2,144,768]{2,1,0:T(8,128)(2,1)S(1)}, u32[]{:S(2)}, u32[]{:S(2)}) collective-permute-start(bf16[2,144,768]{2,1,0:T(8,128)(2,1)S(1)} %shard_map.367.up_own), channel_id=1, source_target_pairs={{0,8},{1,17},{2,10},{3,19},{4,12},{5,21},{6,14},{7,23},{8,0},{9,25... | collective-permute-start | bytes 1327112 | tf_op jit(solution)/shard_map/ppermute | solution.py:595
  140.4 6.3 %collective-permute-start.30 = (bf16[80,768]{1,0:T(8,128)(2,1)S(1)}, bf16[80,768]{1,0:T(8,128)(2,1)S(1)}, u32[]{:S(2)}, u32[]{:S(2)}) collective-permute-start(bf16[80,768]{1,0:T(8,128)(2,1)S(1)} %shard_map.362.own), channel_id=1, source_target_pairs={{0,16},{1,9},{2,18},{3,11},{4,20},{5,13},{6,22},{7,15},{8,24},{9,1... | collective-permute-start | bytes 368648 | tf_op jit(solution)/shard_map/ppermute | solution.py:595
  141.4 8.5 %collective-permute-start.29 = (bf16[2,80,768]{2,1,0:T(8,128)(2,1)S(1)}, bf16[2,80,768]{2,1,0:T(8,128)(2,1)S(1)}, u32[]{:S(2)}, u32[]{:S(2)}) collective-permute-start(bf16[2,80,768]{2,1,0:T(8,128)(2,1)S(1)} %shard_map.365.own), channel_id=1, source_target_pairs={{0,8},{1,17},{2,10},{3,19},{4,12},{5,21},{6,14},{7,23},{8,0},{9,25... | collective-permute-start | bytes 737288 | tf_op jit(solution)/shard_map/ppermute | solution.py:595
  146.7 6.3 %collective-permute-start.32 = (bf16[2,80,768]{2,1,0:T(8,128)(2,1)S(1)}, bf16[2,80,768]{2,1,0:T(8,128)(2,1)S(1)}, u32[]{:S(2)}, u32[]{:S(2)}) collective-permute-start(bf16[2,80,768]{2,1,0:T(8,128)(2,1)S(1)} %shard_map.368.down_own), channel_id=1, source_target_pairs={{0,8},{1,17},{2,10},{3,19},{4,12},{5,21},{6,14},{7,23},{8,0},{9,25... | collective-permute-start | bytes 737288 | tf_op jit(solution)/shard_map/ppermute | solution.py:595
  (24 other events, 225.3 us)
